TPU v7x, 512 devices: a whole 4x8x8 slice. The times are simulated.
512 devices in a mesh: dp: 128 (over z, y, core), tp: 4 (over x).
Axes of the slice: x: 4, y: 8, z: 8, core: 2. Of those that a mesh axis runs over, the one named last changes fastest.
Arguments:
- queries: bfloat16 [2, 128, 8192], P(None, 'dp', 'tp'), may hold values from -8 to 8
- new_token_keys: bfloat16 [2, 128, 512], P(None, 'dp', 'tp'), may hold values from -6 to 6
- new_token_values: bfloat16 [2, 128, 512], P(None, 'dp', 'tp'), may hold values from -6 to 6
- key_pool: bfloat16 [8192, 128, 512], P('dp', None, 'tp'), may hold values from -8 to 8
- value_pool: bfloat16 [8192, 128, 512], P('dp', None, 'tp'), may hold values from -6 to 6
- block_list: int32 [2, 4096, 2], P(None, ('dp', 'tp')), may hold values from 0 to 127, as said below
- context_len: int32 [2, 128], P(None, 'dp'), may hold values from 1 to 4096, as said below
Outputs:
- attn_out: bfloat16 [2, 128, 8192], P(None, 'dp', 'tp')
Inputs may be any that keep to these rules, and one draw needn't show every extreme that they name: `block_list`: each entry is (holder rank, pool slot). Every slot of every holder holds exactly one block of one micro-batch. On one holder, the blocks of one rank's requests over both micro-batches number 0 or 2; the bound 2 is also reached within a single micro-batch. Cached tokens, the new token aside. For every rank and micro-batch, ceil(context_len / 128) summed over the rank's 1 request is 32.
All inputs are finite; a program needn't handle non-finite values.
Results may differ from a plain program's by a relative error of at most 0.011.
Values may be sent and summed in bfloat16 or wider, within the bound.
No kernel may reach another device: no remote copies, remote signals or barrier semaphores. Data moves between devices by JAX's collectives and lax.ppermute only.
A program may use at most 64 MiB of HBM per device.

v0:
```python
from functools import partial

import jax
import jax.numpy as jnp
from jax import lax
from jax.sharding import PartitionSpec as P


def block_terms(query_row_list, key_row_list, value_row_list, live_tokens):
    score_scale = query_row_list.shape[-1] ** (-0.5)
    scores = (
        jnp.einsum("ehd,ebd->ehb", query_row_list, key_row_list, preferred_element_type=jnp.float32)
        * score_scale
    )
    live_mask = (
        lax.broadcasted_iota(jnp.int32, scores.shape, 2)
        < jnp.maximum(live_tokens, 1)[:, None, None]
    )
    scores = jnp.where(live_mask, scores, -1e30)
    peak_score = jnp.max(scores, axis=2)
    weight = jnp.where(live_mask, jnp.exp(scores - peak_score[:, :, None]), 0.0)
    weight_sum = jnp.sum(weight, axis=2)
    mixed_sum = jnp.einsum(
        "ehb,ebd->ehd",
        weight.astype(jnp.bfloat16),
        value_row_list,
        preferred_element_type=jnp.float32,
    )
    return ((mixed_sum / weight_sum[:, :, None]).astype(jnp.bfloat16), peak_score, weight_sum)


def block_requests(block_rows, lengths, block_len):
    block_count = block_rows.shape[0]
    sizes_of = (lengths + block_len - 1) // block_len
    block_ends = jnp.cumsum(sizes_of)
    block_starts = block_ends - sizes_of
    position = jnp.arange(block_count, dtype=jnp.int32)
    request = jnp.sum((position[:, None] >= block_ends[None, :]).astype(jnp.int32), axis=1)
    chosen = request[:, None] == jnp.arange(lengths.shape[0], dtype=jnp.int32)[None, :]
    first_block = jnp.sum(jnp.where(chosen, block_starts[None, :], 0), axis=1)
    span_tokens = jnp.sum(jnp.where(chosen, lengths[None, :], 0), axis=1)
    return (request, jnp.clip(span_tokens - (position - first_block) * block_len, 0, block_len))


def slot_layout(block_all, lens_all, members, my_rank, slot_count, block_len, row_count):
    spread = lens_all.shape[1] // row_count
    group_rows = len(members) * row_count
    slot_ids = jnp.arange(slot_count, dtype=jnp.int32)
    slot_row = jnp.zeros((slot_count,), jnp.int32)
    slot_live = jnp.zeros((slot_count,), jnp.int32)
    slot_hits = jnp.zeros((slot_count,), jnp.int32)
    finder = partial(block_requests, block_len=block_len)
    for offset, index in enumerate(members):
        blocks = block_all[index].reshape(spread, -1, 2)
        request, live = jax.vmap(finder)(blocks, lens_all[index].reshape(spread, row_count))
        owner_ids = lax.broadcasted_iota(jnp.int32, request.shape, 0)
        target = owner_ids * group_rows + offset * row_count + request
        match = (blocks[:, :, 0] == my_rank)[:, :, None] & (
            blocks[:, :, 1][:, :, None] == slot_ids[None, None, :]
        )
        slot_row = slot_row + jnp.sum(jnp.where(match, target[:, :, None], 0), axis=(0, 1))
        slot_live = slot_live + jnp.sum(jnp.where(match, live[:, :, None], 0), axis=(0, 1))
        slot_hits = slot_hits + jnp.sum(match.astype(jnp.int32), axis=(0, 1))
    return (slot_row, slot_live, slot_hits > 0)


def per_device(
    queries, new_token_keys, new_token_values, key_pool, value_pool, block_list, context_len
):
    spread = lax.axis_size("dp")
    micro_count, row_count, feature_width = queries.shape
    slot_count, block_len, head_dim = key_pool.shape
    head_count = feature_width // head_dim
    block_table = lax.all_gather(block_list, "tp", axis=1, tiled=True)
    query_head_rows = queries.reshape(micro_count, row_count, head_count, head_dim)
    block_all, lens_all = (
        lax.all_gather(block_table, "dp", axis=1, tiled=True),
        lax.all_gather(context_len, "dp", axis=1, tiled=True),
    )
    my_rank = lax.axis_index("dp")
    rounds = [list(range(micro_count))]
    results = []
    for members in rounds:
        stacked = query_head_rows.reshape(len(members) * row_count, feature_width)
        group_rows = len(members) * row_count
        rows_total = spread * group_rows
        score_scale = head_dim ** (-0.5)
        everyone = lax.all_gather(stacked, "dp", axis=0, tiled=True)
        slot_row, slot_live, active = slot_layout(
            block_all, lens_all, members, my_rank, slot_count, block_len, row_count
        )
        asked = jnp.take(everyone, slot_row, axis=0).reshape(slot_count, head_count, head_dim)
        partial_out, peak_score, weight_sum = block_terms(asked, key_pool, value_pool, slot_live)
        onehot = (slot_row[None, :] == jnp.arange(rows_total, dtype=jnp.int32)[:, None]) & active[
            None, :
        ]
        local_peak = jnp.max(jnp.where(onehot[:, :, None], peak_score[None], -1e30), axis=1)
        key_row_list = new_token_keys.reshape(group_rows, head_dim)
        value_row_list = new_token_values.reshape(group_rows, head_dim)
        own_score = (
            jnp.einsum(
                "rhd,rd->rh",
                stacked.reshape(group_rows, head_count, head_dim),
                key_row_list,
                preferred_element_type=jnp.float32,
            )
            * score_scale
        )
        own_full = jnp.where(
            jnp.arange(spread, dtype=jnp.int32)[:, None, None] == my_rank, own_score[None], -1e30
        ).reshape(rows_total, head_count)
        ceiling_all = lax.pmax(jnp.maximum(local_peak, own_full), "dp")
        slot_ceiling = jnp.take(ceiling_all, slot_row, axis=0)
        slot_weight = jnp.where(
            active[:, None], jnp.exp(peak_score - slot_ceiling) * weight_sum, 0.0
        )
        selector = onehot.astype(jnp.float32)
        weighted = (slot_weight[:, :, None] * partial_out.astype(jnp.float32)).reshape(
            slot_count, feature_width
        )
        numer_all = jnp.dot(selector, weighted, precision=lax.Precision.HIGHEST)
        denom_all = jnp.dot(selector, slot_weight, precision=lax.Precision.HIGHEST)
        numer_mine, denom_mine = (
            lax.psum_scatter(
                numer_all.reshape(spread, group_rows, feature_width),
                "dp",
                scatter_dimension=0,
                tiled=True,
            ),
            lax.psum_scatter(
                denom_all.reshape(spread, group_rows, head_count),
                "dp",
                scatter_dimension=0,
                tiled=True,
            ),
        )
        ceiling_mine = lax.dynamic_index_in_dim(
            ceiling_all.reshape(spread, group_rows, head_count), my_rank, 0, keepdims=False
        )
        self_weight = jnp.exp(own_score - ceiling_mine)
        numerator = numer_mine.reshape(group_rows, head_count, head_dim) + self_weight[
            :, :, None
        ] * value_row_list[:, None, :].astype(jnp.float32)
        denominator = denom_mine.reshape(group_rows, head_count) + self_weight
        merged = (
            (numerator / denominator[:, :, None])
            .astype(jnp.bfloat16)
            .reshape(group_rows, feature_width)
        )
        for offset in range(len(members)):
            results.append(merged[offset * row_count : (offset + 1) * row_count])
        continue
    return jnp.stack(results)


def solution(mesh):
    placed = (
        P(None, "dp", "tp"),
        P(None, "dp", "tp"),
        P(None, "dp", "tp"),
        P("dp", None, "tp"),
        P("dp", None, "tp"),
        P(None, ("dp", "tp"), None),
        P(None, "dp"),
    )
    return jax.shard_map(
        per_device, mesh=mesh, in_specs=placed, out_specs=P(None, "dp", "tp"), check_vma=False
    )
```

profile of v0, /device:TPU:2, one launch (start us, length us, event | category | flops | bytes accessed | tf_op | source)
XLA Modules:
  0.0 1154.4 jit_solution(10866390371244066478)
XLA Ops:
  6.5 1.5 copy.29
  8.1 50.6 %all-gather.1 = s32[128,1,2]{2,1,0:T(1,128)S(1)} all-gather(s32[1,1,2]{2,1,0:T(1,128)} %bitcast.77), channel_id=1, replica_groups=mesh['dp'=128,'tp'=4] {'dp'}, dimensions={0}, use_global_device_ids=true | all-gather | bytes 1032 | tf_op jit(solution)/shard_map/all_gather | solution.py:78
  58.7 0.2 slice_reduce_fusion
  58.9 0.8 copy.22
  59.6 12.0 %all_gather.12 = s32[2,32,2]{2,0,1:T(2,128)S(1)} all-gather(s32[2,8,2]{2,0,1:T(2,128)S(1)} %copy.22), channel_id=1, replica_groups=mesh['dp'=128,'tp'=4] {'tp'}, dimensions={1}, use_global_device_ids=true | all-gather | bytes 640 | tf_op jit(solution)/shard_map/all_gather | solution.py:74
  71.6 50.7 %all_gather.13 = s32[2,4096,2]{2,0,1:T(2,128)S(1)} all-gather(s32[2,32,2]{2,0,1:T(2,128)S(1)} %all_gather.12), channel_id=1, replica_groups=mesh['dp'=128,'tp'=4] {'dp'}, dimensions={1}, use_global_device_ids=true | all-gather | bytes 66048 | tf_op jit(solution)/shard_map/all_gather | solution.py:77
  122.3 4.1 fusion.32
  126.4 2.7 fusion.34
  129.1 2.4 copy.39
  131.5 4.9 fusion.33
  136.4 2.4 copy.41
  139.0 2.7 copy.44
  141.7 2.7 copy.43
  144.5 0.1 broadcast_in_dim.187
  144.7 0.5 convert_reduce_fusion
  145.2 0.5 convert_reduce_fusion.1
  146.0 2.2 copy.56
  148.2 0.7 gather_fusion
  149.2 1.3 fusion.36
  150.4 0.2 select_reduce_fusion
  150.9 493.6 %pmax.7 = f32[256,16]{1,0:T(8,128)S(1)} all-reduce(f32[256,16]{1,0:T(8,128)S(1)} %select_maximum_fusion), channel_id=1, replica_groups=mesh['dp'=128,'tp'=4] {'dp'}, use_global_device_ids=true, to_apply=%region_8.9 | all-reduce | flops 4096 | bytes 32768 | tf_op jit(solution)/shard_map/pmax | solution.py:112
  644.5 0.6 gather_fusion.1
  645.1 0.4 fusion.7
  645.7 2.2 fusion.3
  647.9 1.1 fusion.13
  649.0 2.9 copy.31
  652.0 1.3 dynamic-slice
  653.3 0.4 fusion.29
  653.6 491.1 %all-reduce.1 = f32[128,2,16]{2,1,0:T(2,128)S(1)} all-reduce(f32[128,2,16]{2,1,0:T(2,128)S(1)} %bitcast.70), channel_id=4, replica_groups=mesh['dp'=128,'tp'=4] {'dp'}, use_global_device_ids=true, to_apply=%region_11.12.clone | all-reduce | flops 4096 | bytes 32768
  1144.7 0.7 fusion.24
  1145.4 1.4 dynamic-slice_bitcast_fusion
  1146.9 0.6 pad_maximum_fusion
  (45 shorter events, 1.4 us)
Async XLA Ops:
  6.5 142.6 %copy-start = (bf16[64,128,128]{2,1,0:T(8,128)(2,1)S(1)}, bf16[64,128,128]{2,1,0:T(8,128)(2,1)}, u32[]{:S(2)}) copy-start(bf16[64,128,128]{2,1,0:T(8,128)(2,1)} %param.10) | copy-start | bytes 6291460
  6.5 139.5 %all-gather.4.cloned.1.call-start = ((), (), s32[]{:S(2)}) async-start(), calls=%async_computation | async-start | bytes 2113536 | tf_op jit(solution)/shard_map/all_gather | solution.py:88
  8.0 1137.4 %all-reduce.4.cloned.1.call-start = ((), (), s32[]{:S(2)}) async-start(), calls=%async_computation.1 | async-start | bytes 4194304
  138.9 6.8 copy-start.1
  139.0 6.8 copy-start.2
  651.9 1.3 copy-start.3
Sparse Core Ops, SparseCore 0:
  10.5 87.5 all-gather.3
  652.1 194.6 all-reduce.3
where the time goes:
time: 1150 us
  blocking collectives  1100 us (96%)
  local copies, waits for them, and re-layouts  34 us (3%)
  between operations  13.7 us (1%)
    pmax x1, blocking collectives, per_device(): ceiling_all = lax.pmax(jnp.maximum(local_peak, own_full), 'dp')  494 us
    unnamed x1, blocking collectives  491 us
    all_gather x1, blocking collectives, per_device(): lax.all_gather(block_table, 'dp', axis=1, tiled=True)  50.7 us
    all_gather x1, blocking collectives, per_device(): lax.all_gather(context_len, 'dp', axis=1, tiled=True)  50.6 us
  transfers between devices with their start and end apart: 2, of which 0 were waited for; matrix products, arithmetic and copies ran while one was open for 2% of the time, Pallas kernels for 0%

commit v1 on v0

v1 whole, which is shorter than its diff:
```python
import functools

import jax
import jax.numpy as jnp
from jax import lax
from jax.experimental import pallas as pl
from jax.experimental.pallas import tpu as pltpu
from jax.sharding import Mesh, PartitionSpec as P

LANES = 128
META = 8
EMPTY = -1e30
PARTS = 3
F32, BF16 = jnp.float32, jnp.bfloat16


def lane_ids(shape):
    return lax.broadcasted_iota(jnp.int32, shape, len(shape) - 1)


def split3(x):
    high = x.astype(BF16).astype(F32)
    rest = x - high
    middle = rest.astype(BF16).astype(F32)
    return high, middle, rest - middle


def joined(tile):
    axis = tile.ndim - 1
    return tile + pltpu.roll(tile, LANES - 1, axis) + pltpu.roll(tile, LANES - 2, axis)


def holder_kernel(
    heads, scale, me, own_ref, sib_ref, key_ref, value_ref, mine_ref, theirs_ref,
    asked, keys, values, parts, table, found, spots, sems, spot_sem,
):
    ranks, rows, _ = asked.shape
    half = ranks // 2
    slots, block_len, _ = keys.shape
    entries = slots
    per_micro = entries // 2
    loads = [
        pltpu.make_async_copy(own_ref, asked.at[pl.ds(0, half)], sems.at[0]),
        pltpu.make_async_copy(sib_ref, asked.at[pl.ds(half, half)], sems.at[1]),
        pltpu.make_async_copy(key_ref, keys, sems.at[2]),
        pltpu.make_async_copy(value_ref, values, sems.at[3]),
    ]
    for load in loads:
        load.start()
    parts[:, : 2 * heads, :] = jnp.zeros((ranks, 2 * heads, LANES), BF16)
    parts[:, 2 * heads :, :] = jnp.full((ranks, META, LANES), EMPTY, BF16)
    loads[0].wait()
    loads[1].wait()
    table[...] = asked[:, 2 * heads :, :].astype(F32).reshape(ranks * META, LANES)
    listed = table[pl.ds(0, ranks, stride=META), :]
    tails = table[pl.ds(1, ranks, stride=META), :]
    lane = lane_ids((ranks, LANES))
    here = (listed == me[0].astype(F32)) & (lane < entries)
    slot = pltpu.roll(listed, LANES // 2, 1)
    code = slot * entries + lane.astype(F32)
    first = jnp.min(jnp.where(here, code, 1e6), axis=1, keepdims=True)
    last = jnp.max(jnp.where(here, code, -1.0), axis=1, keepdims=True)
    valid = last >= 0.0
    row = lax.broadcasted_iota(jnp.int32, (ranks, ranks), 0)
    column = lax.broadcasted_iota(jnp.int32, (ranks, ranks), 1)
    before = jnp.dot(
        (column < row).astype(F32).astype(BF16),
        jnp.broadcast_to(valid.astype(F32), (ranks, LANES)).astype(BF16),
        preferred_element_type=F32,
    )
    chosen = valid & (before == lane.astype(F32))
    rank = lax.broadcasted_iota(jnp.int32, (ranks, LANES), 0).astype(F32)
    tail0 = jnp.sum(jnp.where(lane == 0, tails, 0.0), axis=1, keepdims=True)
    tail1 = jnp.sum(jnp.where(lane == 1, tails, 0.0), axis=1, keepdims=True)

    def listing(x):
        return jnp.sum(jnp.where(chosen, x, 0.0), axis=0, keepdims=True)

    lines = [listing(x) for x in (rank, first, last, tail0, tail1)]
    lines.append(jnp.zeros((8 - len(lines), LANES), F32))
    found[...] = jnp.concatenate(lines, axis=0).astype(jnp.int32)
    move = pltpu.make_async_copy(found, spots, spot_sem)
    move.start()
    move.wait()
    loads[2].wait()
    loads[3].wait()

    pairs = slots // 2
    together = min(4, pairs)
    token = lane_ids((heads, block_len))
    lane8 = lane_ids((8, LANES))

    def step(i, carry):
        work = []
        for k in range(together):
            n = i * together + k
            where = spots[0, n]
            for line in (1, 2):
                block = spots[line, n]
                place = block // entries
                at = block % entries
                micro = at // per_micro
                tail = jnp.where(micro == 0, spots[3, n], spots[4, n])
                live = jnp.where(at % per_micro == per_micro - 1, tail, block_len)
                work.append((where, place, micro, live))
        scores = []
        for where, place, micro, live in work:
            query = asked[where, pl.ds(pl.multiple_of(micro * heads, heads), heads), :]
            score = lax.dot_general(
                query, keys[place], (((1,), (1,)), ((), ())), preferred_element_type=F32
            )
            scores.append(jnp.where(token < live, score * scale, EMPTY))
        score = jnp.concatenate(scores, axis=0)
        peak = jnp.max(score, axis=1, keepdims=True)
        weight = jnp.exp(score - peak)
        total = jnp.sum(weight, axis=1, keepdims=True)
        weight = weight.astype(BF16)
        share = 1.0 / total
        level = peak + jnp.log(total)
        outs = []
        for k, (where, place, micro, live) in enumerate(work):
            mixed = jnp.dot(
                weight[k * heads : (k + 1) * heads], values[place], preferred_element_type=F32
            )
            outs.append(mixed * share[k * heads : (k + 1) * heads])
        for k in range(together):
            where, _, micro_a, _ = work[2 * k]
            _, _, micro_b, _ = work[2 * k + 1]
            level_a = level[2 * k * heads : (2 * k + 1) * heads]
            level_b = level[(2 * k + 1) * heads : (2 * k + 2) * heads]
            tile = jnp.zeros((8, LANES), F32)
            for micro in range(2):
                in_a = (micro_a == micro).astype(F32)
                in_b = (micro_b == micro).astype(F32)
                la = jnp.where(micro_a == micro, level_a, EMPTY)
                lb = jnp.where(micro_b == micro, level_b, EMPTY)
                top = jnp.maximum(la, lb)
                wa = jnp.exp(la - top) * in_a
                wb = jnp.exp(lb - top) * in_b
                both = jnp.maximum(wa + wb, 1e-30)
                part = (outs[2 * k] * wa + outs[2 * k + 1] * wb) / both
                parts[where, micro * heads : (micro + 1) * heads, :] = part.astype(BF16)
                depth = top + jnp.maximum(jnp.log(both), -80.0)
                for piece in range(heads // 8):
                    group = micro * (heads // 8) + piece
                    for j, term in enumerate(split3(depth[piece * 8 : (piece + 1) * 8])):
                        tile = jnp.where(lane8 == PARTS * group + j, term, tile)
            parts[where, 2 * heads :, :] = tile.astype(BF16)
        return carry

    lax.fori_loop(0, pairs // together, step, 0)
    stores = [
        pltpu.make_async_copy(parts.at[pl.ds(half, half)], theirs_ref, sems.at[0]),
        pltpu.make_async_copy(parts.at[pl.ds(0, half)], mine_ref, sems.at[1]),
    ]
    for store in stores:
        store.start()
    for store in stores:
        store.wait()


def merge_kernel(heads, chunk, a_ref, b_ref, out_ref):
    count = a_ref.shape[0]
    groups = 2 * heads // 8
    lane = lane_ids((chunk, 8, LANES))

    def step(i, carry):
        at = pl.ds(i * chunk, chunk)
        la = joined(a_ref[at, 2 * heads :, :].astype(F32))
        lb = joined(b_ref[at, 2 * heads :, :].astype(F32))
        top = jnp.maximum(la, lb)
        wa, wb = jnp.exp(la - top), jnp.exp(lb - top)
        both = wa + wb
        share = wa / both
        depth = top + jnp.log(both)
        depth_tile = jnp.zeros((chunk, 8, LANES), F32)
        terms = split3(depth)
        for j, term in enumerate(terms):
            moved = term if j == 0 else pltpu.roll(term, j, 2)
            depth_tile = jnp.where(lane % PARTS == j, moved, depth_tile)
        out_ref[at, 2 * heads :, :] = jnp.where(
            lane < PARTS * groups, depth_tile, 0.0
        ).astype(BF16)
        a = a_ref[at, : 2 * heads, :].astype(F32)
        b = b_ref[at, : 2 * heads, :].astype(F32)
        scale = jnp.concatenate(
            [
                jnp.broadcast_to(
                    share[:, :, PARTS * g : PARTS * g + 1], (chunk, 8, LANES)
                )
                for g in range(groups)
            ],
            axis=1,
        )
        out_ref[at, : 2 * heads, :] = (b + scale * (a - b)).astype(BF16)
        return carry

    lax.fori_loop(0, count // chunk, step, 0)


def owner_kernel(heads, scale, part_ref, query_ref, key_ref, value_ref, out_ref):
    count = part_ref.shape[0]
    pieces = heads // 8
    groups = 2 * pieces
    lane = lane_ids((8, LANES))
    query = query_ref[...].astype(F32)
    own = jnp.zeros((8, LANES), F32)
    for g in range(groups):
        micro = g // pieces
        key = key_ref[micro : micro + 1, :].astype(F32)
        score = jnp.sum(query[g * 8 : (g + 1) * 8] * key, axis=1, keepdims=True) * scale
        own = jnp.where(lane == PARTS * g, score, own)
    level = joined(part_ref[:, 2 * heads :, :].astype(F32))
    top = jnp.maximum(jnp.max(level, axis=0), own)
    weight = jnp.exp(level - top[None])
    self_weight = jnp.exp(own - top)
    total = jnp.sum(weight, axis=0) + self_weight
    for g in range(groups):
        micro, piece = g // pieces, g % pieces
        if piece == 0:
            rows = part_ref[:, micro * heads : (micro + 1) * heads, :].astype(F32)
        at = PARTS * g
        column = jnp.broadcast_to(weight[:, :, at : at + 1], (count, 8, LANES))
        mixed = jnp.sum(column * rows[:, piece * 8 : (piece + 1) * 8, :], axis=0)
        value = value_ref[micro : micro + 1, :].astype(F32)
        mixed = mixed + self_weight[:, at : at + 1] * value
        out_ref[g * 8 : (g + 1) * 8, :] = mixed / total[:, at : at + 1]


def exchange(x, axis):
    return lax.all_to_all(x, axis, 0, 0)


def per_device(
    queries, new_token_keys, new_token_values, key_pool, value_pool, block_list, context_len
):
    planes, tensor = lax.axis_size("zy"), lax.axis_size("tp")
    micros, _, width = queries.shape
    slots, block_len, dim = key_pool.shape
    heads = width // dim
    scale = dim ** (-0.5)
    rows = micros * heads + META
    swap = [(0, 1), (1, 0)]
    any_space = pl.BlockSpec(memory_space=pl.ANY)
    vmem = pl.BlockSpec(memory_space=pltpu.VMEM)
    params = pltpu.CompilerParams(vmem_limit_bytes=40 * 1024 * 1024)
    message = jax.ShapeDtypeStruct((planes, rows, LANES), BF16)

    with jax.named_scope("entries_over_tp"):
        quarter = block_list.reshape(1, 1, -1).astype(BF16)
        size = quarter.shape[-1]
        quarter = jnp.pad(quarter, ((0, 0), (0, 7), (0, LANES - size)))
        quarters = exchange(jnp.broadcast_to(quarter, (tensor, 8, LANES)), "tp")
        listed = quarters[:, 0, :size].reshape(tensor, micros, -1, 2)
        listed = listed.transpose(3, 1, 0, 2).reshape(2, slots)
        listed = jnp.pad(listed, ((0, 0), (0, LANES // 2 - slots))).reshape(1, LANES)
    with jax.named_scope("queries_to_holders"):
        query = queries.reshape(micros * heads, dim)
        tail = context_len.reshape(1, micros) - (slots // micros - 1) * block_len
        tail = jnp.pad(tail.astype(BF16), ((0, META - 2), (0, LANES - micros)))
        packed = jnp.concatenate([query, listed, tail], axis=0)
        own = exchange(jnp.broadcast_to(packed[None], (planes, rows, LANES)), "zy")
        sibling = lax.ppermute(own, "c", swap)
    with jax.named_scope("block_attention"):
        me = (lax.axis_index("zy") * 2 + lax.axis_index("c")).astype(jnp.int32).reshape(1)
        ranks = 2 * planes
        mine, theirs = pl.pallas_call(
            functools.partial(holder_kernel, heads, scale),
            out_shape=(message, message),
            in_specs=[pl.BlockSpec(memory_space=pltpu.SMEM)] + [any_space] * 4,
            out_specs=(any_space, any_space),
            scratch_shapes=[
                pltpu.VMEM((ranks, rows, LANES), BF16),
                pltpu.VMEM(key_pool.shape, BF16),
                pltpu.VMEM(value_pool.shape, BF16),
                pltpu.VMEM((ranks, rows, LANES), BF16),
                pltpu.VMEM((ranks * META, LANES), F32),
                pltpu.VMEM((8, LANES), jnp.int32),
                pltpu.SMEM((8, LANES), jnp.int32),
                pltpu.SemaphoreType.DMA((4,)),
                pltpu.SemaphoreType.DMA,
            ],
            compiler_params=params,
        )(me, own, sibling, key_pool, value_pool)
    with jax.named_scope("parts_to_owners"):
        other = lax.ppermute(theirs, "c", swap)
        merged = pl.pallas_call(
            functools.partial(merge_kernel, heads, min(8, planes)),
            out_shape=message,
            in_specs=[vmem, vmem],
            out_specs=vmem,
            compiler_params=params,
        )(mine, other)
        arrived = exchange(merged, "zy")
    with jax.named_scope("owner_sum"):
        out = pl.pallas_call(
            functools.partial(owner_kernel, heads, scale),
            out_shape=jax.ShapeDtypeStruct((micros * heads, dim), F32),
            in_specs=[vmem] * 4,
            out_specs=vmem,
            compiler_params=params,
        )(arrived, query, new_token_keys.reshape(micros, dim), new_token_values.reshape(micros, dim))
        return out.astype(BF16).reshape(micros, 1, width)


def solution(mesh):
    spread, tensor = mesh.devices.shape
    finer = Mesh(mesh.devices.reshape(spread // 2, 2, tensor), ("zy", "c", "tp"))
    dp = ("zy", "c")
    placed = (
        P(None, dp, "tp"),
        P(None, dp, "tp"),
        P(None, dp, "tp"),
        P(dp, None, "tp"),
        P(dp, None, "tp"),
        P(None, ("zy", "c", "tp"), None),
        P(None, dp),
    )
    return jax.shard_map(
        per_device, mesh=finer, in_specs=placed, out_specs=P(None, dp, "tp"), check_vma=False
    )
```

time: 1150 us -> 94.9 us (0.08)
  the two profiles are of different devices: /device:TPU:2 before, /device:TPU:8 now
where the time goes in v1:
time: 94.9 us; the launch traced here: 94.5 us
  blocking collectives  64.2 us (68%)
  Pallas kernels  8.38 us (9%)
  starting transfers between devices  8.24 us (9%)
  waiting for transfers between devices  7.95 us (8%)
  local copies, waits for them, and re-layouts  4.14 us (4%)
  other arithmetic  1.51 us (2%)
    all_to_all x2, blocking collectives, exchange(): return lax.all_to_all(x, axis, 0, 0)  64.2 us
    pallas_call x1, Pallas kernels, per_device(): pl.pallas_call(functools.partial(holder_kernel, heads, scale), out_shape=...  6.09 us
    all_to_all x1, starting transfers between devices, exchange(): return lax.all_to_all(x, axis, 0, 0)  4.29 us
    all_to_all x1, waiting for transfers between devices, exchange(): return lax.all_to_all(x, axis, 0, 0)  3.95 us
    ppermute x1, waiting for transfers between devices, per_device(): sibling = lax.ppermute(own, 'c', swap)  2.06 us
    ppermute x1, starting transfers between devices, per_device(): other = lax.ppermute(theirs, 'c', swap)  2.04 us
    ppermute x1, waiting for transfers between devices, per_device(): other = lax.ppermute(theirs, 'c', swap)  1.94 us
    ppermute x1, starting transfers between devices, per_device(): sibling = lax.ppermute(own, 'c', swap)  1.91 us
  transfers between devices with their start and end apart: 3, of which 3 were waited for; matrix products, arithmetic and copies ran while one was open for 1% of the time, Pallas kernels for 0%

profile of v1, /device:TPU:8, one launch (start us, length us, event | category | flops | bytes accessed | tf_op | source)
XLA Modules:
  0.0 94.5 jit_solution(10628402424725810628)
XLA Ops:
  0.0 0.0 copy-start
  0.0 0.8 convert_element_type.35
  0.8 0.1 copy.12
  0.9 0.1 convert_element_type.36
  1.1 0.6 broadcast_in_dim.14
  1.7 4.3 %all-to-all-start = ((bf16[4,8,128]{2,1,0:T(8,128)(2,1)}), bf16[4,8,128]{2,1,0:T(8,128)(2,1)S(1)}, u32[]{:S(2)}, u32[]{:S(2)}) async-start(bf16[4,8,128]{2,1,0:T(8,128)(2,1)} %broadcast_in_dim.14), calls=%async_computation | async-start | bytes 16384 | tf_op jit(solution)/shard_map/entries_over_tp/all_to_all | solution.py:231
  6.0 0.7 convert_bitcast_fusion
  6.6 0.7 reshape.56.query_ref
  7.3 3.9 %all-to-all-done = bf16[4,8,128]{2,1,0:T(8,128)(2,1)S(1)} async-done(((bf16[4,8,128]{2,1,0:T(8,128)(2,1)}), bf16[4,8,128]{2,1,0:T(8,128)(2,1)S(1)}, u32[]{:S(2)}, u32[]{:S(2)}) %all-to-all-start) | async-done | bytes 8224 | tf_op jit(solution)/shard_map/entries_over_tp/all_to_all | solution.py:231
  11.3 0.1 copy.15
  11.4 0.1 copy.14
  11.5 0.1 reshape.57
  11.6 0.1 broadcast_in_dim.15
  11.7 37.0 %all_to_all.15.own_ref = bf16[64,40,128]{2,1,0:T(8,128)(2,1)S(1)} all-to-all(bf16[64,40,128]{2,1,0:T(8,128)(2,1)S(1)} %broadcast_in_dim.15), channel_id=1, replica_groups=mesh['zy'=64,'c'=2,'tp'=4] {'zy'}, dimensions={0} | all-to-all | bytes 1310720 | tf_op jit(solution)/shard_map/queries_to_holders/all_to_all | solution.py:231
  48.8 1.9 %collective-permute-start = (bf16[64,40,128]{2,1,0:T(8,128)(2,1)S(1)}, bf16[64,40,128]{2,1,0:T(8,128)(2,1)S(1)}, u32[]{:S(2)}, u32[]{:S(2)}) collective-permute-start(bf16[64,40,128]{2,1,0:T(8,128)(2,1)S(1)} %all_to_all.15.own_ref), channel_id=1, source_target_pairs={{0,4},{4,0},{1,5},{5,1},{2,6},{6,2},{3,7},{7,3},{8,12},{12,8},{9,1... | collective-permute-start | bytes 1966088 | tf_op jit(solution)/shard_map/queries_to_holders/ppermute | solution.py:263
  50.7 2.1 %collective-permute-done.sib_ref = bf16[64,40,128]{2,1,0:T(8,128)(2,1)S(1)} collective-permute-done((bf16[64,40,128]{2,1,0:T(8,128)(2,1)S(1)}, bf16[64,40,128]{2,1,0:T(8,128)(2,1)S(1)}, u32[]{:S(2)}, u32[]{:S(2)}) %collective-permute-start) | collective-permute-done | bytes 655392 | tf_op jit(solution)/shard_map/queries_to_holders/ppermute | solution.py:263
  52.7 0.0 copy-done
  52.7 0.0 copy-start.1
  52.7 1.6 %copy-done.1 = bf16[64,128,128]{2,1,0:T(8,128)(2,1)S(1)} copy-done((bf16[64,128,128]{2,1,0:T(8,128)(2,1)S(1)}, bf16[64,128,128]{2,1,0:T(8,128)(2,1)}, u32[]{:S(2)}) %copy-start.1) | copy-done | bytes 2097176
  54.3 6.1 %block_attention.1 = (bf16[64,40,128]{2,1,0:T(8,128)(2,1)S(1)}, bf16[64,40,128]{2,1,0:T(8,128)(2,1)S(1)}) custom-call(s32[1]{0:T(128)} %bitcast.me, bf16[64,40,128]{2,1,0:T(8,128)(2,1)S(1)} %all_to_all.15.own_ref, bf16[64,40,128]{2,1,0:T(8,128)(2,1)S(1)} %collective-permute-done.sib_ref, bf16[64,128,128]{2,1,0:T(8,128)(2,1)S(1)} %copy-done, ...), custom_call_target="tpu_custom_call" | custom-call | tf_op jit(solution)/shard_map/block_attention/pallas_call | solution.py:267
  60.4 0.0 copy-start.2
  60.4 0.0 copy-start.3
  60.4 2.0 %collective-permute-start.1 = (bf16[64,40,128]{2,1,0:T(8,128)(2,1)S(1)}, bf16[64,40,128]{2,1,0:T(8,128)(2,1)S(1)}, u32[]{:S(2)}, u32[]{:S(2)}) collective-permute-start(bf16[64,40,128]{2,1,0:T(8,128)(2,1)S(1)} %get-tuple-element.8), channel_id=1, source_target_pairs={{0,4},{4,0},{1,5},{5,1},{2,6},{6,2},{3,7},{7,3},{8,12},{12,8},{9,1... | collective-permute-start | bytes 1966088 | tf_op jit(solution)/shard_map/parts_to_owners/ppermute | solution.py:286
  62.5 1.9 %collective-permute-done.1.b_ref = bf16[64,40,128]{2,1,0:T(8,128)(2,1)S(1)} collective-permute-done((bf16[64,40,128]{2,1,0:T(8,128)(2,1)S(1)}, bf16[64,40,128]{2,1,0:T(8,128)(2,1)S(1)}, u32[]{:S(2)}, u32[]{:S(2)}) %collective-permute-start.1) | collective-permute-done | bytes 655392 | tf_op jit(solution)/shard_map/parts_to_owners/ppermute | solution.py:286
  64.4 1.8 %parts_to_owners.1 = bf16[64,40,128]{2,1,0:T(8,128)(2,1)S(1)} custom-call(bf16[64,40,128]{2,1,0:T(8,128)(2,1)S(1)} %get-tuple-element.7.a_ref, bf16[64,40,128]{2,1,0:T(8,128)(2,1)S(1)} %collective-permute-done.1.b_ref), custom_call_target="tpu_custom_call" | custom-call | tf_op jit(solution)/shard_map/parts_to_owners/pallas_call | solution.py:287
  66.2 27.2 %all_to_all.16.part_ref = bf16[64,40,128]{2,1,0:T(8,128)(2,1)S(1)} all-to-all(bf16[64,40,128]{2,1,0:T(8,128)(2,1)S(1)} %parts_to_owners.1), channel_id=1, replica_groups=mesh['zy'=64,'c'=2,'tp'=4] {'zy'}, dimensions={0} | all-to-all | bytes 1310720 | tf_op jit(solution)/shard_map/parts_to_owners/all_to_all | solution.py:231
  93.4 0.0 copy-done.2
  93.4 0.0 copy-done.3
  93.4 0.5 owner_sum.1
  93.9 0.6 reshape.60
  (4 shorter events, 0.0 us)
Async XLA Ops:
  0.0 52.7 %copy-start = (bf16[64,128,128]{2,1,0:T(8,128)(2,1)S(1)}, bf16[64,128,128]{2,1,0:T(8,128)(2,1)}, u32[]{:S(2)}) copy-start(bf16[64,128,128]{2,1,0:T(8,128)(2,1)} %key_ref.1) | copy-start | bytes 6291460
  1.7 9.6 %all-to-all-start = ((bf16[4,8,128]{2,1,0:T(8,128)(2,1)}), bf16[4,8,128]{2,1,0:T(8,128)(2,1)S(1)}, u32[]{:S(2)}, u32[]{:S(2)}) async-start(bf16[4,8,128]{2,1,0:T(8,128)(2,1)} %broadcast_in_dim.14), calls=%async_computation | async-start | bytes 16384 | tf_op jit(solution)/shard_map/entries_over_tp/all_to_all | solution.py:231
  48.8 4.0 %collective-permute-start = (bf16[64,40,128]{2,1,0:T(8,128)(2,1)S(1)}, bf16[64,40,128]{2,1,0:T(8,128)(2,1)S(1)}, u32[]{:S(2)}, u32[]{:S(2)}) collective-permute-start(bf16[64,40,128]{2,1,0:T(8,128)(2,1)S(1)} %all_to_all.15.own_ref), channel_id=1, source_target_pairs={{0,4},{4,0},{1,5},{5,1},{2,6},{6,2},{3,7},{7,3},{8,12},{12,8},{9,1... | collective-permute-start | bytes 1966088 | tf_op jit(solution)/shard_map/queries_to_holders/ppermute | solution.py:263
  52.7 1.6 %copy-start.1 = (bf16[64,128,128]{2,1,0:T(8,128)(2,1)S(1)}, bf16[64,128,128]{2,1,0:T(8,128)(2,1)}, u32[]{:S(2)}) copy-start(bf16[64,128,128]{2,1,0:T(8,128)(2,1)} %value_ref.1) | copy-start | bytes 6291460
  60.4 33.0 %copy-start.2 = (bf16[2,1,128]{2,0,1:T(2,128)(2,1)S(1)}, bf16[2,1,128]{2,0,1:T(2,128)(2,1)}, u32[]{:S(2)}) copy-start(bf16[2,1,128]{2,0,1:T(2,128)(2,1)} %param.8) | copy-start | bytes 1540
  60.4 33.0 %copy-start.3 = (bf16[2,1,128]{2,0,1:T(2,128)(2,1)S(1)}, bf16[2,1,128]{2,0,1:T(2,128)(2,1)}, u32[]{:S(2)}) copy-start(bf16[2,1,128]{2,0,1:T(2,128)(2,1)} %param.9) | copy-start | bytes 1540
  60.4 4.0 %collective-permute-start.1 = (bf16[64,40,128]{2,1,0:T(8,128)(2,1)S(1)}, bf16[64,40,128]{2,1,0:T(8,128)(2,1)S(1)}, u32[]{:S(2)}, u32[]{:S(2)}) collective-permute-start(bf16[64,40,128]{2,1,0:T(8,128)(2,1)S(1)} %get-tuple-element.8), channel_id=1, source_target_pairs={{0,4},{4,0},{1,5},{5,1},{2,6},{6,2},{3,7},{7,3},{8,12},{12,8},{9,1... | collective-permute-start | bytes 1966088 | tf_op jit(solution)/shard_map/parts_to_owners/ppermute | solution.py:286

commit v2 on v1

v2 whole, which is shorter than its diff:
```python
import functools

import jax
import jax.numpy as jnp
from jax import lax
from jax.experimental import pallas as pl
from jax.experimental.pallas import tpu as pltpu
from jax.sharding import Mesh, PartitionSpec as P

LANES = 128
FIELD = 16
SPAN = 32
EMPTY = -1e30
PARTS = 3
F32, BF16 = jnp.float32, jnp.bfloat16


def lane_ids(shape):
    return lax.broadcasted_iota(jnp.int32, shape, len(shape) - 1)


def split3(x):
    high = x.astype(BF16).astype(F32)
    rest = x - high
    middle = rest.astype(BF16).astype(F32)
    return high, middle, rest - middle


def joined(row):
    return row + pltpu.roll(row, LANES - 1, 1) + pltpu.roll(row, LANES - 2, 1)


def turned(tile, back):
    sublane = lax.broadcasted_iota(jnp.int32, tile.shape, 0)
    for bit in (1, 2, 4):
        shift = bit * FIELD
        moved = pltpu.roll(tile, LANES - shift if back else shift, 1)
        tile = jnp.where((sublane & bit) != 0, moved, tile)
    return tile


def to_row(tile):
    return jnp.sum(turned(tile, False), axis=0, keepdims=True)


def to_tile(row):
    return turned(jnp.broadcast_to(row, (8, LANES)), True)


def column(tile, group):
    at = PARTS * group
    return jnp.broadcast_to(tile[:, at : at + 1], (8, LANES))


def pack_kernel(first_tail, query_ref, list_ref, length_ref, out_ref, wide, rows):
    heads, micros, _ = query_ref.shape
    per = list_ref.shape[2]
    wide[...] = query_ref[...].astype(F32)
    query = jnp.concatenate([wide[:, m, :] for m in range(micros)], axis=0).astype(BF16)
    rows[...] = jnp.zeros(rows.shape, F32)
    for m in range(micros):
        rows[2 * m : 2 * m + 2, :per] = list_ref[m].astype(F32)
    rows[2 * micros : 2 * micros + 1, :micros] = (length_ref[...] - first_tail).astype(F32)
    listed = rows[2 * micros : 2 * micros + 1, :]
    listed = pltpu.roll(listed, 2 * FIELD, 1)
    for m in range(micros):
        for field in range(2):
            at = 2 * m + field
            shift = field * FIELD + m * per
            row = rows[at : at + 1, :]
            listed = listed + (pltpu.roll(row, shift, 1) if shift else row)
    listed = jnp.concatenate([listed, jnp.zeros((1, LANES), F32)], axis=0).astype(BF16)
    message = jnp.concatenate([query.reshape(heads, micros, LANES), listed[None]], axis=0)
    out_ref[...] = jnp.broadcast_to(message[None], out_ref.shape)


def holder_kernel(
    heads, scale, tensor, per, me, own_ref, sib_ref, entry_ref, key_ref, value_ref,
    mine_ref, theirs_ref, keys, values, found, spots, sems, spot_sem,
):
    half = own_ref.shape[0]
    ranks = 2 * half
    slots, block_len, _ = keys.shape
    entries = slots
    per_micro = entries // 2
    loads = [
        pltpu.make_async_copy(key_ref, keys, sems.at[0]),
        pltpu.make_async_copy(value_ref, values, sems.at[1]),
    ]
    for load in loads:
        load.start()

    core = me[0] % 2
    lane = lane_ids((ranks, LANES))
    quarters = []
    for t in range(tensor):
        quarters.append(
            jnp.concatenate(
                [
                    entry_ref[core * tensor + t].astype(F32),
                    entry_ref[(1 - core) * tensor + t].astype(F32),
                ],
                axis=0,
            )
        )
    tails = quarters[0]
    listed = jnp.zeros((ranks, LANES), F32)
    for t, quarter in enumerate(quarters):
        moved = pltpu.roll(quarter, t * SPAN, 1) if t else quarter
        listed = jnp.where(lane // SPAN == t, moved, listed)
    index = lane % FIELD
    order = (index // (per // 2)) * per_micro + (lane // SPAN) * (per // 2) + index % (per // 2)
    here = (listed == me[0].astype(F32)) & (lane % SPAN < per) & (lane < tensor * SPAN)
    slot = pltpu.roll(listed, LANES - FIELD, 1)
    code = slot * entries + order.astype(F32)
    first = jnp.min(jnp.where(here, code, 1e6), axis=1, keepdims=True)
    last = jnp.max(jnp.where(here, code, -1.0), axis=1, keepdims=True)
    valid = last >= 0.0
    row = lax.broadcasted_iota(jnp.int32, (ranks, ranks), 0)
    ahead = lax.broadcasted_iota(jnp.int32, (ranks, ranks), 1)
    before = jnp.dot(
        (ahead < row).astype(F32).astype(BF16),
        jnp.broadcast_to(valid.astype(F32), (ranks, LANES)).astype(BF16),
        preferred_element_type=F32,
    )
    chosen = valid & (before == lane.astype(F32))
    rank = lax.broadcasted_iota(jnp.int32, (ranks, LANES), 0).astype(F32)
    tail0 = jnp.sum(jnp.where(lane == 2 * FIELD, tails, 0.0), axis=1, keepdims=True)
    tail1 = jnp.sum(jnp.where(lane == 2 * FIELD + 1, tails, 0.0), axis=1, keepdims=True)

    def listing(x):
        return jnp.sum(jnp.where(chosen, x, 0.0), axis=0, keepdims=True)

    lines = [listing(x) for x in (rank, first, last, tail0, tail1)]
    lines.append(jnp.zeros((8 - len(lines), LANES), F32))
    found[...] = jnp.concatenate(lines, axis=0).astype(jnp.int32)
    move = pltpu.make_async_copy(found, spots, spot_sem)
    move.start()
    for ref in (mine_ref, theirs_ref):
        ref[:, :heads] = jnp.zeros((half, heads, 2, LANES), BF16)
        ref[:, heads] = jnp.full((half, 2, LANES), EMPTY, BF16)
    move.wait()
    for load in loads:
        load.wait()

    pairs = slots // 2
    together = min(4, pairs)
    token = lane_ids((heads, block_len))
    lane8 = lane_ids((8, LANES))

    def step(i, carry):
        work = []
        for k in range(together):
            n = i * together + k
            where = spots[0, n]
            for line in (1, 2):
                block = spots[line, n]
                place = block // entries
                at = block % entries
                micro = at // per_micro
                tail = jnp.where(micro == 0, spots[3, n], spots[4, n])
                live = jnp.where(at % per_micro == per_micro - 1, tail, block_len)
                work.append((where, place, micro, live))
        scores = []
        for where, place, micro, live in work:
            inner = pl.ds(micro * (heads // 2), heads // 2)
            query = jnp.where(
                where < half, own_ref[where % half, inner], sib_ref[where % half, inner]
            ).reshape(heads, LANES)
            score = lax.dot_general(
                query, keys[place], (((1,), (1,)), ((), ())), preferred_element_type=F32
            )
            scores.append(jnp.where(token < live, score * scale, EMPTY))
        score = jnp.concatenate(scores, axis=0)
        peak = jnp.max(score, axis=1, keepdims=True)
        weight = jnp.exp(score - peak)
        total = jnp.sum(weight, axis=1, keepdims=True)
        weight = weight.astype(BF16)
        share = 1.0 / total
        level = peak + jnp.log(total)
        outs = []
        for k, (where, place, micro, live) in enumerate(work):
            mixed = jnp.dot(
                weight[k * heads : (k + 1) * heads], values[place], preferred_element_type=F32
            )
            outs.append(mixed * share[k * heads : (k + 1) * heads])
        for k in range(together):
            where, _, micro_a, _ = work[2 * k]
            _, _, micro_b, _ = work[2 * k + 1]
            level_a = level[2 * k * heads : (2 * k + 1) * heads]
            level_b = level[(2 * k + 1) * heads : (2 * k + 2) * heads]
            tile = jnp.zeros((8, LANES), F32)
            rows = []
            for micro in range(2):
                in_a = (micro_a == micro).astype(F32)
                in_b = (micro_b == micro).astype(F32)
                la = jnp.where(micro_a == micro, level_a, EMPTY)
                lb = jnp.where(micro_b == micro, level_b, EMPTY)
                top = jnp.maximum(la, lb)
                wa = jnp.exp(la - top) * in_a
                wb = jnp.exp(lb - top) * in_b
                both = jnp.maximum(wa + wb, 1e-30)
                part = (outs[2 * k] * wa + outs[2 * k + 1] * wb) / both
                rows.append(part)
                depth = top + jnp.maximum(jnp.log(both), -80.0)
                for piece in range(heads // 8):
                    group = micro * (heads // 8) + piece
                    for j, term in enumerate(split3(depth[piece * 8 : (piece + 1) * 8])):
                        tile = jnp.where(lane8 == PARTS * group + j, term, tile)
            depths = jnp.concatenate([to_row(tile), jnp.zeros((1, LANES), F32)], axis=0)
            part = jnp.concatenate(rows, axis=0).astype(BF16).reshape(heads, 2, LANES)
            for ref, chosen_here in ((mine_ref, where < half), (theirs_ref, where >= half)):

                @pl.when(chosen_here)
                def _():
                    ref[where % half, :heads] = part
                    ref[where % half, heads] = depths.astype(BF16)

        return carry

    lax.fori_loop(0, pairs // together, step, 0)


def merge_kernel(heads, a_ref, b_ref, out_ref, shares):
    count = a_ref.shape[0]
    groups = 2 * heads // 8
    lane = lane_ids((2 * count, LANES)) % FIELD
    la = joined(a_ref[:, heads].astype(F32).reshape(2 * count, LANES))
    lb = joined(b_ref[:, heads].astype(F32).reshape(2 * count, LANES))
    top = jnp.maximum(la, lb)
    wa, wb = jnp.exp(la - top), jnp.exp(lb - top)
    both = wa + wb
    shares[...] = wa / both
    depth = top + jnp.log(both)
    row = jnp.zeros(depth.shape, F32)
    for j, term in enumerate(split3(depth)):
        moved = pltpu.roll(term, j, 1) if j else term
        row = jnp.where((lane % PARTS == j) & (lane < PARTS * groups), moved, row)
    out_ref[:, heads] = row.astype(BF16).reshape(count, 2, LANES)

    def step(e, carry):
        tile = to_tile(shares[pl.ds(2 * e, 1), :])
        scale = jnp.concatenate([column(tile, g) for g in range(groups)], axis=0)
        a = a_ref[e, :heads].reshape(2 * heads, LANES).astype(F32)
        b = b_ref[e, :heads].reshape(2 * heads, LANES).astype(F32)
        out_ref[e, :heads] = (b + scale * (a - b)).astype(BF16).reshape(heads, 2, LANES)
        return carry

    lax.fori_loop(0, count, step, 0, unroll=min(8, count))


def owner_kernel(heads, scale, part_ref, query_ref, key_ref, value_ref, out_ref, weights, wide):
    count = part_ref.shape[0]
    pieces = heads // 8
    groups = 2 * pieces
    lane = lane_ids((8, LANES))
    wide[...] = query_ref[...].astype(F32)
    own = jnp.zeros((8, LANES), F32)
    for g in range(groups):
        micro, piece = g // pieces, g % pieces
        query = wide[piece * 8 : (piece + 1) * 8, micro, :]
        key = key_ref[micro : micro + 1, :].astype(F32)
        score = jnp.sum(query * key, axis=1, keepdims=True) * scale
        own = jnp.where(lane == PARTS * g, score, own)
    own = to_row(own)
    level = joined(part_ref[:, heads].astype(F32).reshape(2 * count, LANES))
    line = lax.broadcasted_iota(jnp.int32, level.shape, 0)
    level = jnp.where(line % 2 == 0, level, EMPTY)
    top = jnp.maximum(jnp.max(level, axis=0, keepdims=True), own)
    weight = jnp.exp(level - top)
    weights[...] = weight
    self_weight = jnp.exp(own - top)
    total = to_tile(jnp.sum(weight, axis=0, keepdims=True) + self_weight)
    self_weight = to_tile(self_weight)

    def step(e, mixed):
        tile = to_tile(weights[pl.ds(2 * e, 1), :])
        scale = jnp.concatenate([column(tile, g) for g in range(groups)], axis=0)
        return mixed + scale * part_ref[e, :heads].reshape(2 * heads, LANES).astype(F32)

    mixed = lax.fori_loop(
        0, count, step, jnp.zeros((2 * heads, LANES), F32), unroll=min(8, count)
    )
    for g in range(groups):
        micro, piece = g // pieces, g % pieces
        value = value_ref[micro : micro + 1, :].astype(F32)
        part = mixed[g * 8 : (g + 1) * 8] + column(self_weight, g) * value
        wide[piece * 8 : (piece + 1) * 8, micro, :] = part / column(total, g)
    out_ref[...] = wide[...].astype(BF16)


def exchange(x, axis):
    return lax.all_to_all(x, axis, 0, 0)


def per_device(
    queries, new_token_keys, new_token_values, key_pool, value_pool, block_list, context_len
):
    planes, tensor = lax.axis_size("zy"), lax.axis_size("tp")
    micros, _, width = queries.shape
    slots, block_len, dim = key_pool.shape
    heads = width // dim
    scale = dim ** (-0.5)
    per = slots // tensor
    swap = [(0, 1), (1, 0)]
    hbm = pl.BlockSpec(memory_space=pltpu.HBM)
    vmem = pl.BlockSpec(memory_space=pltpu.VMEM)
    params = pltpu.CompilerParams(vmem_limit_bytes=32 * 1024 * 1024)
    message = jax.ShapeDtypeStruct((planes, heads + 1, micros, LANES), BF16)
    query = queries.reshape(micros, heads, dim).transpose(1, 0, 2)

    with jax.named_scope("queries_to_holders"):
        packed = pl.pallas_call(
            functools.partial(pack_kernel, (slots // micros - 1) * block_len),
            out_shape=message,
            in_specs=[vmem] * 3,
            out_specs=vmem,
            scratch_shapes=[pltpu.VMEM(query.shape, F32), pltpu.VMEM((8, LANES), F32)],
            compiler_params=params,
        )(query, block_list.transpose(0, 2, 1), context_len.transpose(1, 0))
        own = exchange(packed, "zy")
        sibling = lax.ppermute(own, "c", swap)
        rows = own[:, heads, 0]
        rows = exchange(
            jnp.broadcast_to(rows[None], (2 * tensor, planes, LANES)), ("c", "tp")
        )
    with jax.named_scope("block_attention"):
        me = (lax.axis_index("zy") * 2 + lax.axis_index("c")).astype(jnp.int32).reshape(1)
        mine, theirs = pl.pallas_call(
            functools.partial(holder_kernel, heads, scale, tensor, per),
            out_shape=(message, message),
            in_specs=[pl.BlockSpec(memory_space=pltpu.SMEM)] + [vmem] * 3 + [hbm] * 2,
            out_specs=(vmem, vmem),
            scratch_shapes=[
                pltpu.VMEM(key_pool.shape, BF16),
                pltpu.VMEM(value_pool.shape, BF16),
                pltpu.VMEM((8, LANES), jnp.int32),
                pltpu.SMEM((8, LANES), jnp.int32),
                pltpu.SemaphoreType.DMA((2,)),
                pltpu.SemaphoreType.DMA,
            ],
            compiler_params=params,
        )(me, own, sibling, rows, key_pool, value_pool)
    with jax.named_scope("parts_to_owners"):
        other = lax.ppermute(theirs, "c", swap)
        merged = pl.pallas_call(
            functools.partial(merge_kernel, heads),
            out_shape=message,
            in_specs=[vmem, vmem],
            out_specs=vmem,
            scratch_shapes=[pltpu.VMEM((2 * planes, LANES), F32)],
            compiler_params=params,
        )(mine, other)
        arrived = exchange(merged, "zy")
    with jax.named_scope("owner_sum"):
        out = pl.pallas_call(
            functools.partial(owner_kernel, heads, scale),
            out_shape=jax.ShapeDtypeStruct(query.shape, BF16),
            in_specs=[vmem] * 4,
            out_specs=vmem,
            scratch_shapes=[
                pltpu.VMEM((2 * planes, LANES), F32),
                pltpu.VMEM(query.shape, F32),
            ],
            compiler_params=params,
        )(arrived, query, new_token_keys.reshape(micros, dim), new_token_values.reshape(micros, dim))
        return out.transpose(1, 0, 2).reshape(micros, 1, width)


def solution(mesh):
    spread, tensor = mesh.devices.shape
    finer = Mesh(mesh.devices.reshape(spread // 2, 2, tensor), ("zy", "c", "tp"))
    dp = ("zy", "c")
    placed = (
        P(None, dp, "tp"),
        P(None, dp, "tp"),
        P(None, dp, "tp"),
        P(dp, None, "tp"),
        P(dp, None, "tp"),
        P(None, ("zy", "c", "tp"), None),
        P(None, dp),
    )
    return jax.shard_map(
        per_device, mesh=finer, in_specs=placed, out_specs=P(None, dp, "tp"), check_vma=False
    )
```

time: 94.9 us -> 103 us (1.085)
  Pallas kernels: 8.38 us -> 20.3 us
  blocking collectives: 64.2 us -> 61.7 us
  other arithmetic: 1.51 us -> 0 us
    pallas_call x2 -> x3, Pallas kernels: 7.87 us -> 16.5 us  [the longest x1 12.5 us: per_device(): pl.pallas_call(functools.partial(holder_kernel, heads, scale, tensor, per...]
    pallas_call x1, Pallas kernels: 0.51 us -> 3.86 us  [per_device(): pl.pallas_call(functools.partial(owner_kernel, heads, scale), out_shape=j...]
    all_to_all x2, blocking collectives: 64.2 us -> 61.7 us  [exchange(): return lax.all_to_all(x, axis, 0, 0)]
    unnamed x9 -> x17, local copies, waits for them, and re-layouts: 1.71 us -> 3.8 us
    ppermute x1, waiting for transfers between devices: 2.06 us -> 0.01 us  [per_device(): sibling = lax.ppermute(own, 'c', swap)]
    all_to_all x1, waiting for transfers between devices: 3.95 us -> 5.56 us  [exchange(): return lax.all_to_all(x, axis, 0, 0)]
    convert_element_type x3 -> x0, other arithmetic: 1.5 us -> none  [the longest x1 0.83 us: per_device(): quarter = block_list.reshape(1, 1, -1).astype(BF16)]
    reshape x3 -> x0, local copies, waits for them, and re-layouts: 1.42 us -> none  [the longest x1 0.71 us: per_device(): query = queries.reshape(micros * heads, dim)]
  transfers between devices with their start and end apart: 3 -> 3, of which waited for: 3 -> 2; matrix products, arithmetic and copies ran while one was open for 1% -> 1% of each run, Pallas kernels for 0% -> 0%
where the time goes in v2:
time: 103 us; the launch traced here: 102 us
  blocking collectives  61.7 us (60%)
  Pallas kernels  20.3 us (20%)
  starting transfers between devices  8.46 us (8%)
  waiting for transfers between devices  7.38 us (7%)
  local copies, waits for them, and re-layouts  4.49 us (4%)
    all_to_all x2, blocking collectives, exchange(): return lax.all_to_all(x, axis, 0, 0)  61.7 us
    pallas_call x1, Pallas kernels, per_device(): pl.pallas_call(functools.partial(holder_kernel, heads, scale, tensor, per...  12.5 us
    all_to_all x1, waiting for transfers between devices, exchange(): return lax.all_to_all(x, axis, 0, 0)  5.56 us
    all_to_all x1, starting transfers between devices, exchange(): return lax.all_to_all(x, axis, 0, 0)  4.4 us
    pallas_call x1, Pallas kernels, per_device(): pl.pallas_call(functools.partial(owner_kernel, heads, scale), out_shape=j...  3.86 us
    unnamed x17, local copies, waits for them, and re-layouts  3.8 us
    pallas_call x1, Pallas kernels, per_device(): pl.pallas_call(functools.partial(merge_kernel, heads), out_shape=message,...  3.69 us
    ppermute x1, starting transfers between devices, per_device(): other = lax.ppermute(theirs, 'c', swap)  2.15 us
  transfers between devices with their start and end apart: 3, of which 2 were waited for; matrix products, arithmetic and copies ran while one was open for 1% of the time, Pallas kernels for 0%

profile of v2, /device:TPU:8, one launch (start us, length us, event | category | flops | bytes accessed | tf_op | source)
XLA Modules:
  0.0 102.5 jit_solution(10151980947838996162)
XLA Ops:
  0.0 0.0 copy-start
  0.0 0.0 copy-start.2
  0.0 0.8 copy-done.2
  0.8 0.0 copy-start.4
  0.9 0.7 copy-done.4
  1.5 0.0 copy-start.7
  1.5 0.7 copy-done.7
  2.2 0.3 queries_to_holders.1
  2.5 36.5 %all_to_all.15.own_ref = bf16[64,17,2,128]{3,2,1,0:T(2,128)(2,1)S(1)} all-to-all(bf16[64,17,2,128]{3,2,1,0:T(2,128)(2,1)S(1)} %queries_to_holders.1), channel_id=1, replica_groups=mesh['zy'=64,'c'=2,'tp'=4] {'zy'}, dimensions={0} | all-to-all | bytes 1114112 | tf_op jit(solution)/shard_map/queries_to_holders/all_to_all | solution.py:293
  39.0 1.9 %collective-permute-start = (bf16[64,17,2,128]{3,2,1,0:T(2,128)(2,1)S(1)}, bf16[64,17,2,128]{3,2,1,0:T(2,128)(2,1)S(1)}, u32[]{:S(2)}, u32[]{:S(2)}) collective-permute-start(bf16[64,17,2,128]{3,2,1,0:T(2,128)(2,1)S(1)} %all_to_all.15.own_ref), channel_id=1, source_target_pairs={{0,4},{4,0},{1,5},{5,1},{2,6},{6,2},{3,7},{7,3},{8,12},{12,8},{9,1... | collective-permute-start | bytes 1671176 | tf_op jit(solution)/shard_map/queries_to_holders/ppermute | solution.py:322
  40.9 0.7 broadcast_in_dim.8
  41.6 4.4 %all-to-all-start.1 = ((bf16[8,64,128]{2,1,0:T(8,128)(2,1)}), bf16[8,64,128]{2,1,0:T(8,128)(2,1)S(1)}, u32[]{:S(2)}, u32[]{:S(2)}) async-start(bf16[8,64,128]{2,1,0:T(8,128)(2,1)} %broadcast_in_dim.8), calls=%async_computation.1 | async-start | bytes 262144 | tf_op jit(solution)/shard_map/queries_to_holders/all_to_all | solution.py:293
  46.0 5.6 %all-to-all-done.1.entry_ref = bf16[8,64,128]{2,1,0:T(8,128)(2,1)S(1)} async-done(((bf16[8,64,128]{2,1,0:T(8,128)(2,1)}), bf16[8,64,128]{2,1,0:T(8,128)(2,1)S(1)}, u32[]{:S(2)}, u32[]{:S(2)}) %all-to-all-start.1) | async-done | bytes 131104 | tf_op jit(solution)/shard_map/queries_to_holders/all_to_all | solution.py:293
  51.6 0.0 collective-permute-done.sib_ref
  51.6 0.0 copy-done
  51.6 0.0 copy-start.1
  51.6 1.6 %copy-done.1 = bf16[64,128,128]{2,1,0:T(8,128)(2,1)S(1)} copy-done((bf16[64,128,128]{2,1,0:T(8,128)(2,1)S(1)}, bf16[64,128,128]{2,1,0:T(8,128)(2,1)}, u32[]{:S(2)}) %copy-start.1) | copy-done | bytes 2097176
  53.2 12.5 %block_attention.1 = (bf16[64,17,2,128]{3,2,1,0:T(2,128)(2,1)S(1)}, bf16[64,17,2,128]{3,2,1,0:T(2,128)(2,1)S(1)}) custom-call(s32[1]{0:T(128)} %bitcast.me, bf16[64,17,2,128]{3,2,1,0:T(2,128)(2,1)S(1)} %all_to_all.15.own_ref, bf16[64,17,2,128]{3,2,1,0:T(2,128)(2,1)S(1)} %collective-permute-done.sib_ref, bf16[8,64,128]{2,1,0:T(8,128)(2,1)S(1)} %all-to-all-done.1.entry_ref, ...), custom_call_target="tpu_custom_call" | custom-call | tf_op jit(solution)/shard_map/block_attention/pallas_call | solution.py:329
  65.6 0.0 copy-start.3
  65.7 0.0 copy-start.5
  65.7 0.0 copy-start.6
  65.7 2.2 %collective-permute-start.1 = (bf16[64,17,2,128]{3,2,1,0:T(2,128)(2,1)S(1)}, bf16[64,17,2,128]{3,2,1,0:T(2,128)(2,1)S(1)}, u32[]{:S(2)}, u32[]{:S(2)}) collective-permute-start(bf16[64,17,2,128]{3,2,1,0:T(2,128)(2,1)S(1)} %get-tuple-element.8), channel_id=1, source_target_pairs={{0,4},{4,0},{1,5},{5,1},{2,6},{6,2},{3,7},{7,3},{8,12},{12,8},{9,1... | collective-permute-start | bytes 1671176 | tf_op jit(solution)/shard_map/parts_to_owners/ppermute | solution.py:345
  67.8 1.8 %collective-permute-done.1.b_ref = bf16[64,17,2,128]{3,2,1,0:T(2,128)(2,1)S(1)} collective-permute-done((bf16[64,17,2,128]{3,2,1,0:T(2,128)(2,1)S(1)}, bf16[64,17,2,128]{3,2,1,0:T(2,128)(2,1)S(1)}, u32[]{:S(2)}, u32[]{:S(2)}) %collective-permute-start.1) | collective-permute-done | bytes 557088 | tf_op jit(solution)/shard_map/parts_to_owners/ppermute | solution.py:345
  69.7 3.7 %parts_to_owners.1 = bf16[64,17,2,128]{3,2,1,0:T(2,128)(2,1)S(1)} custom-call(bf16[64,17,2,128]{3,2,1,0:T(2,128)(2,1)S(1)} %get-tuple-element.7.a_ref, bf16[64,17,2,128]{3,2,1,0:T(2,128)(2,1)S(1)} %collective-permute-done.1.b_ref), custom_call_target="tpu_custom_call" | custom-call | tf_op jit(solution)/shard_map/parts_to_owners/pallas_call | solution.py:346
  73.4 25.3 %all_to_all.16.part_ref = bf16[64,17,2,128]{3,2,1,0:T(2,128)(2,1)S(1)} all-to-all(bf16[64,17,2,128]{3,2,1,0:T(2,128)(2,1)S(1)} %parts_to_owners.1), channel_id=1, replica_groups=mesh['zy'=64,'c'=2,'tp'=4] {'zy'}, dimensions={0} | all-to-all | bytes 1114112 | tf_op jit(solution)/shard_map/parts_to_owners/all_to_all | solution.py:293
  98.6 0.0 copy-done.3
  98.6 0.0 copy-done.5
  98.6 0.0 copy-done.6
  98.6 3.9 %owner_sum.1 = bf16[16,2,128]{2,1,0:T(2,128)(2,1)} custom-call(bf16[64,17,2,128]{3,2,1,0:T(2,128)(2,1)S(1)} %all_to_all.16.part_ref, bf16[16,2,128]{2,1,0:T(2,128)(2,1)S(1)} %bitcast.15, bf16[2,128]{1,0:T(2,128)(2,1)S(1)} %bitcast.17, bf16[2,128]{1,0:T(2,128)(2,1)S(1)} %bitcast.18), custom_call_target="tpu_custom_call" | custom-call | tf_op jit(solution)/shard_map/owner_sum/pallas_call | solution.py:356
  (2 shorter events, 0.0 us)
Async XLA Ops:
  0.0 51.6 %copy-start = (bf16[64,128,128]{2,1,0:T(8,128)(2,1)S(1)}, bf16[64,128,128]{2,1,0:T(8,128)(2,1)}, u32[]{:S(2)}) copy-start(bf16[64,128,128]{2,1,0:T(8,128)(2,1)} %key_ref.1) | copy-start | bytes 6291460
  0.0 0.8 copy-start.2
  0.8 0.7 copy-start.4
  1.5 0.7 copy-start.7
  39.0 12.6 %collective-permute-start = (bf16[64,17,2,128]{3,2,1,0:T(2,128)(2,1)S(1)}, bf16[64,17,2,128]{3,2,1,0:T(2,128)(2,1)S(1)}, u32[]{:S(2)}, u32[]{:S(2)}) collective-permute-start(bf16[64,17,2,128]{3,2,1,0:T(2,128)(2,1)S(1)} %all_to_all.15.own_ref), channel_id=1, source_target_pairs={{0,4},{4,0},{1,5},{5,1},{2,6},{6,2},{3,7},{7,3},{8,12},{12,8},{9,1... | collective-permute-start | bytes 1671176 | tf_op jit(solution)/shard_map/queries_to_holders/ppermute | solution.py:322
  41.6 10.0 %all-to-all-start.1 = ((bf16[8,64,128]{2,1,0:T(8,128)(2,1)}), bf16[8,64,128]{2,1,0:T(8,128)(2,1)S(1)}, u32[]{:S(2)}, u32[]{:S(2)}) async-start(bf16[8,64,128]{2,1,0:T(8,128)(2,1)} %broadcast_in_dim.8), calls=%async_computation.1 | async-start | bytes 262144 | tf_op jit(solution)/shard_map/queries_to_holders/all_to_all | solution.py:293
  51.6 1.6 %copy-start.1 = (bf16[64,128,128]{2,1,0:T(8,128)(2,1)S(1)}, bf16[64,128,128]{2,1,0:T(8,128)(2,1)}, u32[]{:S(2)}) copy-start(bf16[64,128,128]{2,1,0:T(8,128)(2,1)} %value_ref.1) | copy-start | bytes 6291460
  65.6 33.0 %copy-start.3 = (bf16[2,1,2048]{2,0,1:T(2,128)(2,1)S(1)}, bf16[2,1,2048]{2,0,1:T(2,128)(2,1)}, u32[]{:S(2)}) copy-start(bf16[2,1,2048]{2,0,1:T(2,128)(2,1)} %param.7) | copy-start | bytes 24580
  65.7 33.0 %copy-start.5 = (bf16[2,1,128]{2,0,1:T(2,128)(2,1)S(1)}, bf16[2,1,128]{2,0,1:T(2,128)(2,1)}, u32[]{:S(2)}) copy-start(bf16[2,1,128]{2,0,1:T(2,128)(2,1)} %param.8) | copy-start | bytes 1540
  65.7 33.0 %copy-start.6 = (bf16[2,1,128]{2,0,1:T(2,128)(2,1)S(1)}, bf16[2,1,128]{2,0,1:T(2,128)(2,1)}, u32[]{:S(2)}) copy-start(bf16[2,1,128]{2,0,1:T(2,128)(2,1)} %param.9) | copy-start | bytes 1540
  65.7 4.0 %collective-permute-start.1 = (bf16[64,17,2,128]{3,2,1,0:T(2,128)(2,1)S(1)}, bf16[64,17,2,128]{3,2,1,0:T(2,128)(2,1)S(1)}, u32[]{:S(2)}, u32[]{:S(2)}) collective-permute-start(bf16[64,17,2,128]{3,2,1,0:T(2,128)(2,1)S(1)} %get-tuple-element.8), channel_id=1, source_target_pairs={{0,4},{4,0},{1,5},{5,1},{2,6},{6,2},{3,7},{7,3},{8,12},{12,8},{9,1... | collective-permute-start | bytes 1671176 | tf_op jit(solution)/shard_map/parts_to_owners/ppermute | solution.py:345

commit v3 on v2

--- a/solution.py
+++ b/solution.py
@@ -30,59 +30,47 @@
     return row + pltpu.roll(row, LANES - 1, 1) + pltpu.roll(row, LANES - 2, 1)
 
 
-def turned(tile, back):
-    sublane = lax.broadcasted_iota(jnp.int32, tile.shape, 0)
-    for bit in (1, 2, 4):
-        shift = bit * FIELD
-        moved = pltpu.roll(tile, LANES - shift if back else shift, 1)
-        tile = jnp.where((sublane & bit) != 0, moved, tile)
-    return tile
-
-
-def to_row(tile):
-    return jnp.sum(turned(tile, False), axis=0, keepdims=True)
-
-
-def to_tile(row):
-    return turned(jnp.broadcast_to(row, (8, LANES)), True)
-
-
-def column(tile, group):
-    at = PARTS * group
-    return jnp.broadcast_to(tile[:, at : at + 1], (8, LANES))
-
-
-def pack_kernel(first_tail, query_ref, list_ref, length_ref, out_ref, wide, rows):
+def spread_levels(rows, groups):
+    count = rows.shape[0] // 2
+    line = lax.broadcasted_iota(jnp.int32, (8 * count, 2 * count), 0)
+    source = lax.broadcasted_iota(jnp.int32, (8 * count, 2 * count), 1)
+    pick = (source == (line // 8) * 2).astype(F32).astype(BF16)
+    copies = jnp.dot(pick, rows, preferred_element_type=F32)
+    sublane = lax.broadcasted_iota(jnp.int32, copies.shape, 0) % 8
+    copies = jnp.where(lane_ids(copies.shape) // FIELD == sublane, copies, 0.0).astype(BF16)
+    at = lax.broadcasted_iota(jnp.int32, (LANES, groups * LANES), 0) % FIELD // PARTS
+    group = lane_ids((LANES, groups * LANES)) // LANES
+    add = (at == group).astype(F32).astype(BF16)
+    levels = jnp.dot(copies, add, preferred_element_type=F32)
+    return [levels[:, g * LANES : (g + 1) * LANES] for g in range(groups)]
+
+
+def pack_kernel(per, query_ref, list_ref, out_ref, wide):
     heads, micros, _ = query_ref.shape
-    per = list_ref.shape[2]
     wide[...] = query_ref[...].astype(F32)
     query = jnp.concatenate([wide[:, m, :] for m in range(micros)], axis=0).astype(BF16)
-    rows[...] = jnp.zeros(rows.shape, F32)
+    row = pltpu.roll(list_ref[micros].astype(F32)[:1], 2 * FIELD, 1)
     for m in range(micros):
-        rows[2 * m : 2 * m + 2, :per] = list_ref[m].astype(F32)
-    rows[2 * micros : 2 * micros + 1, :micros] = (length_ref[...] - first_tail).astype(F32)
-    listed = rows[2 * micros : 2 * micros + 1, :]
-    listed = pltpu.roll(listed, 2 * FIELD, 1)
-    for m in range(micros):
+        fields = list_ref[m].astype(F32)
         for field in range(2):
-            at = 2 * m + field
             shift = field * FIELD + m * per
-            row = rows[at : at + 1, :]
-            listed = listed + (pltpu.roll(row, shift, 1) if shift else row)
-    listed = jnp.concatenate([listed, jnp.zeros((1, LANES), F32)], axis=0).astype(BF16)
+            entry = fields[field : field + 1]
+            row = row + (pltpu.roll(entry, shift, 1) if shift else entry)
+    listed = jnp.concatenate([row, jnp.zeros((1, LANES), F32)], axis=0).astype(BF16)
     message = jnp.concatenate([query.reshape(heads, micros, LANES), listed[None]], axis=0)
     out_ref[...] = jnp.broadcast_to(message[None], out_ref.shape)
 
 
 def holder_kernel(
     heads, scale, tensor, per, me, own_ref, sib_ref, entry_ref, key_ref, value_ref,
-    mine_ref, theirs_ref, keys, values, found, spots, sems, spot_sem,
+    mine_ref, theirs_ref, keys, values, parts, tiles, pad, found, spots, sems, spot_sem,
 ):
     half = own_ref.shape[0]
     ranks = 2 * half
     slots, block_len, _ = keys.shape
     entries = slots
     per_micro = entries // 2
+    groups = 2 * heads // 8
     loads = [
         pltpu.make_async_copy(key_ref, keys, sems.at[0]),
         pltpu.make_async_copy(value_ref, values, sems.at[1]),
@@ -136,9 +124,12 @@
     found[...] = jnp.concatenate(lines, axis=0).astype(jnp.int32)
     move = pltpu.make_async_copy(found, spots, spot_sem)
     move.start()
-    for ref in (mine_ref, theirs_ref):
-        ref[:, :heads] = jnp.zeros((half, heads, 2, LANES), BF16)
-        ref[:, heads] = jnp.full((half, 2, LANES), EMPTY, BF16)
+    parts[:, :heads] = jnp.zeros((ranks, heads, 2, LANES), BF16)
+    ours = lane_ids((8, LANES)) // FIELD == lax.broadcasted_iota(jnp.int32, (8, LANES), 0)
+    field = jnp.where(ours, lane_ids((8, LANES)) % FIELD, FIELD)
+    blank = jnp.where(field < PARTS * groups, EMPTY, 0.0)
+    tiles[...] = jnp.broadcast_to(blank[None], (ranks, 8, LANES)).reshape(ranks * 8, LANES)
+    pad[...] = jnp.zeros(pad.shape, F32)
     move.wait()
     for load in loads:
         load.wait()
@@ -146,7 +137,6 @@
     pairs = slots // 2
     together = min(4, pairs)
     token = lane_ids((heads, block_len))
-    lane8 = lane_ids((8, LANES))
 
     def step(i, carry):
         work = []
@@ -200,92 +190,74 @@
                 wa = jnp.exp(la - top) * in_a
                 wb = jnp.exp(lb - top) * in_b
                 both = jnp.maximum(wa + wb, 1e-30)
-                part = (outs[2 * k] * wa + outs[2 * k + 1] * wb) / both
-                rows.append(part)
+                rows.append((outs[2 * k] * wa + outs[2 * k + 1] * wb) / both)
                 depth = top + jnp.maximum(jnp.log(both), -80.0)
                 for piece in range(heads // 8):
                     group = micro * (heads // 8) + piece
                     for j, term in enumerate(split3(depth[piece * 8 : (piece + 1) * 8])):
-                        tile = jnp.where(lane8 == PARTS * group + j, term, tile)
-            depths = jnp.concatenate([to_row(tile), jnp.zeros((1, LANES), F32)], axis=0)
+                        tile = jnp.where(field == PARTS * group + j, term, tile)
+            tiles[pl.ds(pl.multiple_of(where * 8, 8), 8), :] = tile
             part = jnp.concatenate(rows, axis=0).astype(BF16).reshape(heads, 2, LANES)
-            for ref, chosen_here in ((mine_ref, where < half), (theirs_ref, where >= half)):
-
-                @pl.when(chosen_here)
-                def _():
-                    ref[where % half, :heads] = part
-                    ref[where % half, heads] = depths.astype(BF16)
-
+            parts[where, :heads] = part
         return carry
 
     lax.fori_loop(0, pairs // together, step, 0)
-
-
-def merge_kernel(heads, a_ref, b_ref, out_ref, shares):
+    pad[:, 0, :] = jnp.sum(tiles[...].reshape(ranks, 8, LANES), axis=1)
+    parts[:, heads] = pad[...].astype(BF16)
+    stores = [
+        pltpu.make_async_copy(parts.at[pl.ds(half, half)], theirs_ref, sems.at[0]),
+        pltpu.make_async_copy(parts.at[pl.ds(0, half)], mine_ref, sems.at[1]),
+    ]
+    for store in stores:
+        store.start()
+    for store in stores:
+        store.wait()
+
+
+def merge_kernel(heads, a_ref, b_ref, out_ref):
     count = a_ref.shape[0]
     groups = 2 * heads // 8
     lane = lane_ids((2 * count, LANES)) % FIELD
-    la = joined(a_ref[:, heads].astype(F32).reshape(2 * count, LANES))
-    lb = joined(b_ref[:, heads].astype(F32).reshape(2 * count, LANES))
+    rows_a = a_ref[:, heads].reshape(2 * count, LANES)
+    rows_b = b_ref[:, heads].reshape(2 * count, LANES)
+    la, lb = joined(rows_a.astype(F32)), joined(rows_b.astype(F32))
     top = jnp.maximum(la, lb)
-    wa, wb = jnp.exp(la - top), jnp.exp(lb - top)
-    both = wa + wb
-    shares[...] = wa / both
-    depth = top + jnp.log(both)
+    depth = top + jnp.log(jnp.exp(la - top) + jnp.exp(lb - top))
     row = jnp.zeros(depth.shape, F32)
     for j, term in enumerate(split3(depth)):
         moved = pltpu.roll(term, j, 1) if j else term
         row = jnp.where((lane % PARTS == j) & (lane < PARTS * groups), moved, row)
     out_ref[:, heads] = row.astype(BF16).reshape(count, 2, LANES)
-
-    def step(e, carry):
-        tile = to_tile(shares[pl.ds(2 * e, 1), :])
-        scale = jnp.concatenate([column(tile, g) for g in range(groups)], axis=0)
-        a = a_ref[e, :heads].reshape(2 * heads, LANES).astype(F32)
-        b = b_ref[e, :heads].reshape(2 * heads, LANES).astype(F32)
-        out_ref[e, :heads] = (b + scale * (a - b)).astype(BF16).reshape(heads, 2, LANES)
-        return carry
-
-    lax.fori_loop(0, count, step, 0, unroll=min(8, count))
-
-
-def owner_kernel(heads, scale, part_ref, query_ref, key_ref, value_ref, out_ref, weights, wide):
+    spread_a = spread_levels(rows_a, groups)
+    spread_b = spread_levels(rows_b, groups)
+    for g in range(groups):
+        share = 1.0 / (1.0 + jnp.exp(spread_b[g] - spread_a[g]))
+        at = slice(4 * g, 4 * (g + 1))
+        a = a_ref[:, at].reshape(8 * count, LANES).astype(F32)
+        b = b_ref[:, at].reshape(8 * count, LANES).astype(F32)
+        merged = (b + share * (a - b)).astype(BF16)
+        out_ref[:, at] = merged.reshape(count, 4, 2, LANES)
+
+
+def owner_kernel(heads, scale, part_ref, query_ref, key_ref, value_ref, out_ref, wide):
     count = part_ref.shape[0]
     pieces = heads // 8
     groups = 2 * pieces
-    lane = lane_ids((8, LANES))
     wide[...] = query_ref[...].astype(F32)
-    own = jnp.zeros((8, LANES), F32)
+    levels = spread_levels(part_ref[:, heads].reshape(2 * count, LANES), groups)
     for g in range(groups):
         micro, piece = g // pieces, g % pieces
-        query = wide[piece * 8 : (piece + 1) * 8, micro, :]
+        rows = slice(piece * 8, (piece + 1) * 8)
         key = key_ref[micro : micro + 1, :].astype(F32)
-        score = jnp.sum(query * key, axis=1, keepdims=True) * scale
-        own = jnp.where(lane == PARTS * g, score, own)
-    own = to_row(own)
-    level = joined(part_ref[:, heads].astype(F32).reshape(2 * count, LANES))
-    line = lax.broadcasted_iota(jnp.int32, level.shape, 0)
-    level = jnp.where(line % 2 == 0, level, EMPTY)
-    top = jnp.maximum(jnp.max(level, axis=0, keepdims=True), own)
-    weight = jnp.exp(level - top)
-    weights[...] = weight
-    self_weight = jnp.exp(own - top)
-    total = to_tile(jnp.sum(weight, axis=0, keepdims=True) + self_weight)
-    self_weight = to_tile(self_weight)
-
-    def step(e, mixed):
-        tile = to_tile(weights[pl.ds(2 * e, 1), :])
-        scale = jnp.concatenate([column(tile, g) for g in range(groups)], axis=0)
-        return mixed + scale * part_ref[e, :heads].reshape(2 * heads, LANES).astype(F32)
-
-    mixed = lax.fori_loop(
-        0, count, step, jnp.zeros((2 * heads, LANES), F32), unroll=min(8, count)
-    )
-    for g in range(groups):
-        micro, piece = g // pieces, g % pieces
-        value = value_ref[micro : micro + 1, :].astype(F32)
-        part = mixed[g * 8 : (g + 1) * 8] + column(self_weight, g) * value
-        wide[piece * 8 : (piece + 1) * 8, micro, :] = part / column(total, g)
+        own = jnp.sum(wide[rows, micro, :] * key, axis=1, keepdims=True) * scale
+        level = levels[g].reshape(count, 8, LANES)
+        top = jnp.maximum(jnp.max(level, axis=0), own)
+        weight = jnp.exp(level - top[None])
+        self_weight = jnp.exp(own - top)
+        part = part_ref[:, 4 * g : 4 * (g + 1)].reshape(8 * count, LANES).astype(F32)
+        mixed = jnp.sum(weight * part.reshape(count, 8, LANES), axis=0)
+        mixed = mixed + self_weight * value_ref[micro : micro + 1, :].astype(F32)
+        wide[rows, micro, :] = mixed / (jnp.sum(weight, axis=0) + self_weight)
     out_ref[...] = wide[...].astype(BF16)
 
 
@@ -306,18 +278,23 @@
     hbm = pl.BlockSpec(memory_space=pltpu.HBM)
     vmem = pl.BlockSpec(memory_space=pltpu.VMEM)
     params = pltpu.CompilerParams(vmem_limit_bytes=32 * 1024 * 1024)
+    large = pltpu.CompilerParams(vmem_limit_bytes=50 * 1024 * 1024)
     message = jax.ShapeDtypeStruct((planes, heads + 1, micros, LANES), BF16)
     query = queries.reshape(micros, heads, dim).transpose(1, 0, 2)
 
     with jax.named_scope("queries_to_holders"):
+        part = block_list.shape[1]
+        listed = jnp.pad(block_list.transpose(0, 2, 1), ((0, 1), (0, 0), (0, LANES - part)))
+        tails = context_len.transpose(1, 0)[None] - (slots // micros - 1) * block_len
+        listed = listed + jnp.pad(tails, ((micros, 0), (0, 1), (0, LANES - micros)))
         packed = pl.pallas_call(
-            functools.partial(pack_kernel, (slots // micros - 1) * block_len),
+            functools.partial(pack_kernel, part),
             out_shape=message,
-            in_specs=[vmem] * 3,
+            in_specs=[vmem] * 2,
             out_specs=vmem,
-            scratch_shapes=[pltpu.VMEM(query.shape, F32), pltpu.VMEM((8, LANES), F32)],
+            scratch_shapes=[pltpu.VMEM(query.shape, F32)],
             compiler_params=params,
-        )(query, block_list.transpose(0, 2, 1), context_len.transpose(1, 0))
+        )(query, listed)
         own = exchange(packed, "zy")
         sibling = lax.ppermute(own, "c", swap)
         rows = own[:, heads, 0]
@@ -330,16 +307,19 @@
             functools.partial(holder_kernel, heads, scale, tensor, per),
             out_shape=(message, message),
             in_specs=[pl.BlockSpec(memory_space=pltpu.SMEM)] + [vmem] * 3 + [hbm] * 2,
-            out_specs=(vmem, vmem),
+            out_specs=(pl.BlockSpec(memory_space=pl.ANY),) * 2,
             scratch_shapes=[
                 pltpu.VMEM(key_pool.shape, BF16),
                 pltpu.VMEM(value_pool.shape, BF16),
+                pltpu.VMEM((2 * planes, heads + 1, micros, LANES), BF16),
+                pltpu.VMEM((2 * planes * 8, LANES), F32),
+                pltpu.VMEM((2 * planes, 2, LANES), F32),
                 pltpu.VMEM((8, LANES), jnp.int32),
                 pltpu.SMEM((8, LANES), jnp.int32),
                 pltpu.SemaphoreType.DMA((2,)),
                 pltpu.SemaphoreType.DMA,
             ],
-            compiler_params=params,
+            compiler_params=large,
         )(me, own, sibling, rows, key_pool, value_pool)
     with jax.named_scope("parts_to_owners"):
         other = lax.ppermute(theirs, "c", swap)
@@ -348,7 +328,6 @@
             out_shape=message,
             in_specs=[vmem, vmem],
             out_specs=vmem,
-            scratch_shapes=[pltpu.VMEM((2 * planes, LANES), F32)],
             compiler_params=params,
         )(mine, other)
         arrived = exchange(merged, "zy")
@@ -359,7 +338,6 @@
             in_specs=[vmem] * 4,
             out_specs=vmem,
             scratch_shapes=[
-                pltpu.VMEM((2 * planes, LANES), F32),
                 pltpu.VMEM(query.shape, F32),
             ],
             compiler_params=params,

time: 103 us -> 91.3 us (0.89)
  Pallas kernels: 20.3 us -> 10.5 us
  local copies, waits for them, and re-layouts: 4.49 us -> 1.41 us
  other arithmetic: 0 us -> 1.34 us
    pallas_call x1, Pallas kernels: 12.5 us -> 6.41 us  [per_device(): pl.pallas_call(functools.partial(holder_kernel, heads, scale, tensor, per...]
    unnamed x17 -> x9, local copies, waits for them, and re-layouts: 3.8 us -> 0.72 us
    pallas_call x1, Pallas kernels: 3.86 us -> 1.48 us  [per_device(): pl.pallas_call(functools.partial(owner_kernel, heads, scale), out_shape=j...]
    pallas_call x1, Pallas kernels: 3.69 us -> 2.29 us  [per_device(): pl.pallas_call(functools.partial(merge_kernel, heads), out_shape=message,...]
where the time goes in v3:
time: 91.3 us; the launch traced here: 90.9 us
  blocking collectives  61.7 us (68%)
  Pallas kernels  10.5 us (12%)
  starting transfers between devices  8.46 us (9%)
  waiting for transfers between devices  7.38 us (8%)
  local copies, waits for them, and re-layouts  1.41 us (2%)
  other arithmetic  1.34 us (1%)
    all_to_all x2, blocking collectives, exchange(): return lax.all_to_all(x, axis, 0, 0)  61.7 us
    pallas_call x1, Pallas kernels, per_device(): pl.pallas_call(functools.partial(holder_kernel, heads, scale, tensor, per...  6.41 us
    all_to_all x1, waiting for transfers between devices, exchange(): return lax.all_to_all(x, axis, 0, 0)  5.56 us
    all_to_all x1, starting transfers between devices, exchange(): return lax.all_to_all(x, axis, 0, 0)  4.4 us
    pallas_call x1, Pallas kernels, per_device(): pl.pallas_call(functools.partial(merge_kernel, heads), out_shape=message,...  2.29 us
    ppermute x1, starting transfers between devices, per_device(): other = lax.ppermute(theirs, 'c', swap)  2.15 us
    ppermute x1, starting transfers between devices, per_device(): sibling = lax.ppermute(own, 'c', swap)  1.91 us
  transfers between devices with their start and end apart: 3, of which 2 were waited for; matrix products, arithmetic and copies ran while one was open for 1% of the time, Pallas kernels for 0%

profile of v3, /device:TPU:8, one launch (start us, length us, event | category | flops | bytes accessed | tf_op | source)
XLA Modules:
  0.0 90.9 jit_solution(3683880962725114800)
XLA Ops:
  0.0 0.7 add_bitcast_fusion
  0.7 0.7 pad_add_fusion.list_ref
  1.3 0.0 copy-start
  1.3 0.7 copy-done
  2.0 0.3 queries_to_holders.1
  2.4 36.5 %all_to_all.15.own_ref = bf16[64,17,2,128]{3,2,1,0:T(2,128)(2,1)S(1)} all-to-all(bf16[64,17,2,128]{3,2,1,0:T(2,128)(2,1)S(1)} %queries_to_holders.1), channel_id=1, replica_groups=mesh['zy'=64,'c'=2,'tp'=4] {'zy'}, dimensions={0} | all-to-all | bytes 1114112 | tf_op jit(solution)/shard_map/queries_to_holders/all_to_all | solution.py:265
  38.8 1.9 %collective-permute-start = (bf16[64,17,2,128]{3,2,1,0:T(2,128)(2,1)S(1)}, bf16[64,17,2,128]{3,2,1,0:T(2,128)(2,1)S(1)}, u32[]{:S(2)}, u32[]{:S(2)}) collective-permute-start(bf16[64,17,2,128]{3,2,1,0:T(2,128)(2,1)S(1)} %all_to_all.15.own_ref), channel_id=1, source_target_pairs={{0,4},{4,0},{1,5},{5,1},{2,6},{6,2},{3,7},{7,3},{8,12},{12,8},{9,1... | collective-permute-start | bytes 1671176 | tf_op jit(solution)/shard_map/queries_to_holders/ppermute | solution.py:299
  40.8 0.7 broadcast_in_dim.8
  41.5 4.4 %all-to-all-start.1 = ((bf16[8,64,128]{2,1,0:T(8,128)(2,1)}), bf16[8,64,128]{2,1,0:T(8,128)(2,1)S(1)}, u32[]{:S(2)}, u32[]{:S(2)}) async-start(bf16[8,64,128]{2,1,0:T(8,128)(2,1)} %broadcast_in_dim.8), calls=%async_computation.1 | async-start | bytes 262144 | tf_op jit(solution)/shard_map/queries_to_holders/all_to_all | solution.py:265
  45.9 5.6 %all-to-all-done.1.entry_ref = bf16[8,64,128]{2,1,0:T(8,128)(2,1)S(1)} async-done(((bf16[8,64,128]{2,1,0:T(8,128)(2,1)}), bf16[8,64,128]{2,1,0:T(8,128)(2,1)S(1)}, u32[]{:S(2)}, u32[]{:S(2)}) %all-to-all-start.1) | async-done | bytes 131104 | tf_op jit(solution)/shard_map/queries_to_holders/all_to_all | solution.py:265
  51.4 0.0 collective-permute-done.sib_ref
  51.4 6.4 %block_attention.1 = (bf16[64,17,2,128]{3,2,1,0:T(2,128)(2,1)S(1)}, bf16[64,17,2,128]{3,2,1,0:T(2,128)(2,1)S(1)}) custom-call(s32[1]{0:T(128)} %bitcast.me, bf16[64,17,2,128]{3,2,1,0:T(2,128)(2,1)S(1)} %all_to_all.15.own_ref, bf16[64,17,2,128]{3,2,1,0:T(2,128)(2,1)S(1)} %collective-permute-done.sib_ref, bf16[8,64,128]{2,1,0:T(8,128)(2,1)S(1)} %all-to-all-done.1.entry_ref, ...), custom_call_target="tpu_custom_call" | custom-call | tf_op jit(solution)/shard_map/block_attention/pallas_call | solution.py:306
  57.8 0.0 copy-start.1
  57.9 0.0 copy-start.2
  57.9 0.0 copy-start.3
  57.9 2.2 %collective-permute-start.1 = (bf16[64,17,2,128]{3,2,1,0:T(2,128)(2,1)S(1)}, bf16[64,17,2,128]{3,2,1,0:T(2,128)(2,1)S(1)}, u32[]{:S(2)}, u32[]{:S(2)}) collective-permute-start(bf16[64,17,2,128]{3,2,1,0:T(2,128)(2,1)S(1)} %get-tuple-element.8), channel_id=1, source_target_pairs={{0,4},{4,0},{1,5},{5,1},{2,6},{6,2},{3,7},{7,3},{8,12},{12,8},{9,1... | collective-permute-start | bytes 1671176 | tf_op jit(solution)/shard_map/parts_to_owners/ppermute | solution.py:325
  60.0 1.8 %collective-permute-done.1.b_ref = bf16[64,17,2,128]{3,2,1,0:T(2,128)(2,1)S(1)} collective-permute-done((bf16[64,17,2,128]{3,2,1,0:T(2,128)(2,1)S(1)}, bf16[64,17,2,128]{3,2,1,0:T(2,128)(2,1)S(1)}, u32[]{:S(2)}, u32[]{:S(2)}) %collective-permute-start.1) | collective-permute-done | bytes 557088 | tf_op jit(solution)/shard_map/parts_to_owners/ppermute | solution.py:325
  61.9 2.3 %parts_to_owners.1 = bf16[64,17,2,128]{3,2,1,0:T(2,128)(2,1)S(1)} custom-call(bf16[64,17,2,128]{3,2,1,0:T(2,128)(2,1)S(1)} %get-tuple-element.7.a_ref, bf16[64,17,2,128]{3,2,1,0:T(2,128)(2,1)S(1)} %collective-permute-done.1.b_ref), custom_call_target="tpu_custom_call" | custom-call | tf_op jit(solution)/shard_map/parts_to_owners/pallas_call | solution.py:326
  64.2 25.2 %all_to_all.16.part_ref = bf16[64,17,2,128]{3,2,1,0:T(2,128)(2,1)S(1)} all-to-all(bf16[64,17,2,128]{3,2,1,0:T(2,128)(2,1)S(1)} %parts_to_owners.1), channel_id=1, replica_groups=mesh['zy'=64,'c'=2,'tp'=4] {'zy'}, dimensions={0} | all-to-all | bytes 1114112 | tf_op jit(solution)/shard_map/parts_to_owners/all_to_all | solution.py:265
  89.4 0.0 copy-done.1
  89.4 0.0 copy-done.2
  89.4 0.0 copy-done.3
  89.4 1.5 %owner_sum.1 = bf16[16,2,128]{2,1,0:T(2,128)(2,1)} custom-call(bf16[64,17,2,128]{3,2,1,0:T(2,128)(2,1)S(1)} %all_to_all.16.part_ref, bf16[16,2,128]{2,1,0:T(2,128)(2,1)S(1)} %bitcast.16, bf16[2,128]{1,0:T(2,128)(2,1)S(1)} %bitcast.17, bf16[2,128]{1,0:T(2,128)(2,1)S(1)} %bitcast.18), custom_call_target="tpu_custom_call" | custom-call | tf_op jit(solution)/shard_map/owner_sum/pallas_call | solution.py:335
  (2 shorter events, 0.0 us)
Async XLA Ops:
  1.3 0.7 copy-start
  38.8 12.6 %collective-permute-start = (bf16[64,17,2,128]{3,2,1,0:T(2,128)(2,1)S(1)}, bf16[64,17,2,128]{3,2,1,0:T(2,128)(2,1)S(1)}, u32[]{:S(2)}, u32[]{:S(2)}) collective-permute-start(bf16[64,17,2,128]{3,2,1,0:T(2,128)(2,1)S(1)} %all_to_all.15.own_ref), channel_id=1, source_target_pairs={{0,4},{4,0},{1,5},{5,1},{2,6},{6,2},{3,7},{7,3},{8,12},{12,8},{9,1... | collective-permute-start | bytes 1671176 | tf_op jit(solution)/shard_map/queries_to_holders/ppermute | solution.py:299
  41.5 10.0 %all-to-all-start.1 = ((bf16[8,64,128]{2,1,0:T(8,128)(2,1)}), bf16[8,64,128]{2,1,0:T(8,128)(2,1)S(1)}, u32[]{:S(2)}, u32[]{:S(2)}) async-start(bf16[8,64,128]{2,1,0:T(8,128)(2,1)} %broadcast_in_dim.8), calls=%async_computation.1 | async-start | bytes 262144 | tf_op jit(solution)/shard_map/queries_to_holders/all_to_all | solution.py:265
  57.8 31.6 %copy-start.1 = (bf16[2,1,2048]{2,0,1:T(2,128)(2,1)S(1)}, bf16[2,1,2048]{2,0,1:T(2,128)(2,1)}, u32[]{:S(2)}) copy-start(bf16[2,1,2048]{2,0,1:T(2,128)(2,1)} %param.7) | copy-start | bytes 24580
  57.9 31.6 %copy-start.2 = (bf16[2,1,128]{2,0,1:T(2,128)(2,1)S(1)}, bf16[2,1,128]{2,0,1:T(2,128)(2,1)}, u32[]{:S(2)}) copy-start(bf16[2,1,128]{2,0,1:T(2,128)(2,1)} %param.8) | copy-start | bytes 1540
  57.9 31.6 %copy-start.3 = (bf16[2,1,128]{2,0,1:T(2,128)(2,1)S(1)}, bf16[2,1,128]{2,0,1:T(2,128)(2,1)}, u32[]{:S(2)}) copy-start(bf16[2,1,128]{2,0,1:T(2,128)(2,1)} %param.9) | copy-start | bytes 1540
  57.9 4.0 %collective-permute-start.1 = (bf16[64,17,2,128]{3,2,1,0:T(2,128)(2,1)S(1)}, bf16[64,17,2,128]{3,2,1,0:T(2,128)(2,1)S(1)}, u32[]{:S(2)}, u32[]{:S(2)}) collective-permute-start(bf16[64,17,2,128]{3,2,1,0:T(2,128)(2,1)S(1)} %get-tuple-element.8), channel_id=1, source_target_pairs={{0,4},{4,0},{1,5},{5,1},{2,6},{6,2},{3,7},{7,3},{8,12},{12,8},{9,1... | collective-permute-start | bytes 1671176 | tf_op jit(solution)/shard_map/parts_to_owners/ppermute | solution.py:325

commit v4 on v3

v4 whole, which is shorter than its diff:
```python
import functools

import jax
import jax.numpy as jnp
from jax import lax
from jax.experimental import pallas as pl
from jax.experimental.pallas import tpu as pltpu
from jax.sharding import Mesh, PartitionSpec as P

LANES = 128
FIELD = 16
SPAN = 32
EMPTY = -1e30
PARTS = 3
F32, BF16 = jnp.float32, jnp.bfloat16


def lane_ids(shape):
    return lax.broadcasted_iota(jnp.int32, shape, len(shape) - 1)


def split3(x):
    high = x.astype(BF16).astype(F32)
    rest = x - high
    middle = rest.astype(BF16).astype(F32)
    return high, middle, rest - middle


def spread_levels(rows, groups):
    count = rows.shape[0] // 2
    line = lax.broadcasted_iota(jnp.int32, (8 * count, 2 * count), 0)
    source = lax.broadcasted_iota(jnp.int32, (8 * count, 2 * count), 1)
    pick = (source == (line // 8) * 2).astype(F32).astype(BF16)
    copies = jnp.dot(pick, rows, preferred_element_type=F32)
    sublane = lax.broadcasted_iota(jnp.int32, copies.shape, 0) % 8
    copies = jnp.where(lane_ids(copies.shape) // FIELD == sublane, copies, 0.0).astype(BF16)
    at = lax.broadcasted_iota(jnp.int32, (LANES, groups * LANES), 0) % FIELD // PARTS
    group = lane_ids((LANES, groups * LANES)) // LANES
    add = (at == group).astype(F32).astype(BF16)
    levels = jnp.dot(copies, add, preferred_element_type=F32)
    return [levels[:, g * LANES : (g + 1) * LANES] for g in range(groups)]


def pack_kernel(
    first_tail, query_hbm, list_hbm, length_hbm, out_ref, query_ref, list_ref, length_ref,
    wide, rows, sems,
):
    heads, micros, _ = query_ref.shape
    per = list_ref.shape[2]
    loads = [
        pltpu.make_async_copy(query_hbm, query_ref, sems.at[0]),
        pltpu.make_async_copy(list_hbm, list_ref, sems.at[1]),
        pltpu.make_async_copy(length_hbm, length_ref, sems.at[2]),
    ]
    for load in loads:
        load.start()
    rows[...] = jnp.zeros(rows.shape, F32)
    for load in loads:
        load.wait()
    wide[...] = query_ref[...].astype(F32)
    query = jnp.concatenate([wide[:, m, :] for m in range(micros)], axis=0).astype(BF16)
    for m in range(micros):
        rows[2 * m : 2 * m + 2, :per] = list_ref[m].astype(F32)
    rows[2 * micros : 2 * micros + 1, :micros] = (length_ref[...] - first_tail).astype(F32)
    row = pltpu.roll(rows[2 * micros : 2 * micros + 1, :], 2 * FIELD, 1)
    for m in range(micros):
        for field in range(2):
            at = 2 * m + field
            shift = field * FIELD + m * per
            entry = rows[at : at + 1, :]
            row = row + (pltpu.roll(entry, shift, 1) if shift else entry)
    listed = jnp.concatenate([row, jnp.zeros((1, LANES), F32)], axis=0).astype(BF16)
    message = jnp.concatenate([query.reshape(heads, micros, LANES), listed[None]], axis=0)
    out_ref[...] = jnp.broadcast_to(message[None], out_ref.shape)


def holder_kernel(
    heads, scale, tensor, per, me, own_ref, entry_ref, key_ref, value_ref, sib_key_ref,
    sib_value_ref, out_ref, keys, values, mixed, levels, pad, found, spots, sems, spot_sem,
):
    ranks = own_ref.shape[0]
    slots, block_len, _ = keys.shape
    entries = slots
    per_micro = entries // 2
    groups = 2 * heads // 8
    loads = [
        pltpu.make_async_copy(key_ref, keys, sems.at[0]),
        pltpu.make_async_copy(value_ref, values, sems.at[1]),
    ]
    for load in loads:
        load.start()
    pools = ((sib_key_ref, sib_value_ref), (keys, values))

    lane = lane_ids((ranks, LANES))
    listed = jnp.zeros((ranks, LANES), F32)
    for t in range(tensor):
        quarter = entry_ref[t].astype(F32)
        if t == 0:
            tails = quarter
        moved = pltpu.roll(quarter, t * SPAN, 1) if t else quarter
        listed = jnp.where(lane // SPAN == t, moved, listed)
    index = lane % FIELD
    order = (index // (per // 2)) * per_micro + (lane // SPAN) * (per // 2) + index % (per // 2)
    place = (lane % SPAN < per) & (lane < tensor * SPAN)
    slot = pltpu.roll(listed, LANES - FIELD, 1)
    code = slot * entries + order.astype(F32)
    firsts, lasts = [], []
    for holder in (me[0] + 1 - 2 * (me[0] % 2), me[0]):
        here = (listed == holder.astype(F32)) & place
        firsts.append(jnp.min(jnp.where(here, code, 1e6), axis=1, keepdims=True))
        lasts.append(jnp.max(jnp.where(here, code, -1.0), axis=1, keepdims=True))
    second = lane >= LANES // 2
    first = jnp.where(second, firsts[1], firsts[0])
    last = jnp.where(second, lasts[1], lasts[0])
    valid = last >= 0.0
    row = lax.broadcasted_iota(jnp.int32, (ranks, ranks), 0)
    ahead = lax.broadcasted_iota(jnp.int32, (ranks, ranks), 1)
    before = jnp.dot(
        (ahead < row).astype(F32).astype(BF16),
        valid.astype(F32).astype(BF16),
        preferred_element_type=F32,
    )
    chosen = valid & (before == (lane % (LANES // 2)).astype(F32))
    rank = lax.broadcasted_iota(jnp.int32, (ranks, LANES), 0).astype(F32)
    tail0 = jnp.sum(jnp.where(lane == 2 * FIELD, tails, 0.0), axis=1, keepdims=True)
    tail1 = jnp.sum(jnp.where(lane == 2 * FIELD + 1, tails, 0.0), axis=1, keepdims=True)

    def listing(x):
        return jnp.sum(jnp.where(chosen, x, 0.0), axis=0, keepdims=True)

    lines = [listing(x) for x in (rank, first, last, tail0, tail1)]
    lines[0] = jnp.where(listing(1.0) > 0.0, lines[0], float(ranks))
    lines.append(jnp.sum(valid.astype(F32), axis=0, keepdims=True))
    lines.append(jnp.zeros((8 - len(lines), LANES), F32))
    found[...] = jnp.concatenate(lines, axis=0).astype(jnp.int32)
    move = pltpu.make_async_copy(found, spots, spot_sem)
    move.start()
    mixed[...] = jnp.zeros(mixed.shape, F32)
    levels[...] = jnp.full(levels.shape, EMPTY, F32)
    pad[...] = jnp.zeros(pad.shape, F32)
    move.wait()

    together = min(4, slots // 2)
    token = lane_ids((heads, block_len))

    def step(pool, i, carry):
        work = []
        for k in range(together):
            n = pool * (LANES // 2) + i * together + k
            where = spots[0, n]
            for line in (1, 2):
                block = spots[line, n]
                at = block % entries
                micro = at // per_micro
                tail = jnp.where(micro == 0, spots[3, n], spots[4, n])
                live = jnp.where(at % per_micro == per_micro - 1, tail, block_len)
                work.append((where, block // entries, micro, live))
        olds = [(mixed[work[2 * k][0]], levels[work[2 * k][0]]) for k in range(together)]
        scores = []
        for where, block, micro, live in work:
            inner = pl.ds(micro * (heads // 2), heads // 2)
            query = own_ref[jnp.minimum(where, ranks - 1), inner].reshape(heads, LANES)
            score = lax.dot_general(
                query, pools[pool][0][block], (((1,), (1,)), ((), ())), preferred_element_type=F32
            )
            scores.append(jnp.where(token < live, score * scale, EMPTY))
        score = jnp.concatenate(scores, axis=0)
        peak = jnp.max(score, axis=1, keepdims=True)
        weight = jnp.exp(score - peak)
        total = jnp.sum(weight, axis=1, keepdims=True)
        weight = weight.astype(BF16)
        share = 1.0 / total
        level = peak + jnp.log(total)
        outs = []
        for k, (where, block, micro, live) in enumerate(work):
            part = jnp.dot(
                weight[k * heads : (k + 1) * heads],
                pools[pool][1][block],
                preferred_element_type=F32,
            )
            outs.append(part * share[k * heads : (k + 1) * heads])
        news = []
        for k in range(together):
            micro_a, micro_b = work[2 * k][2], work[2 * k + 1][2]
            level_a = level[2 * k * heads : (2 * k + 1) * heads]
            level_b = level[(2 * k + 1) * heads : (2 * k + 2) * heads]
            old_mixed, old_level = olds[k]
            for micro in range(2):
                rows = slice(micro * heads, (micro + 1) * heads)
                la = jnp.where(micro_a == micro, level_a, EMPTY)
                lb = jnp.where(micro_b == micro, level_b, EMPTY)
                top = jnp.maximum(old_level[rows], jnp.maximum(la, lb))
                wo = jnp.exp(old_level[rows] - top)
                wa = jnp.exp(la - top) * (micro_a == micro).astype(F32)
                wb = jnp.exp(lb - top) * (micro_b == micro).astype(F32)
                both = wo + wa + wb
                part = wo * old_mixed[rows] + wa * outs[2 * k] + wb * outs[2 * k + 1]
                news.append((work[2 * k][0], rows, part / both, top + jnp.log(both)))
        for where, rows, part, depth in news:
            mixed[where, rows] = part
            levels[where, rows] = depth
        return carry

    for pool in range(2):
        if pool == 1:
            for load in loads:
                load.wait()
        count = spots[5, pool * (LANES // 2)]
        steps = (count + together - 1) // together
        lax.fori_loop(0, steps, functools.partial(step, pool), 0)

    sublane = lax.broadcasted_iota(jnp.int32, (1, 8, LANES), 1)
    lane8 = lane_ids((1, 8, LANES))
    field = jnp.where(lane8 // FIELD == sublane, lane8 % FIELD, FIELD)
    tile = jnp.zeros((ranks, 8, LANES), F32)
    for g in range(groups):
        for j, term in enumerate(split3(levels[:ranks, 8 * g : 8 * (g + 1)])):
            tile = jnp.where(field == PARTS * g + j, term, tile)
    pad[:, 0, :] = jnp.sum(tile, axis=1)
    out_ref[:, heads] = pad[...].astype(BF16)
    out_ref[:, :heads] = mixed[:ranks].astype(BF16).reshape(ranks, heads, 2, LANES)


def owner_kernel(heads, scale, part_ref, query_ref, key_ref, value_ref, out_ref, wide):
    count = part_ref.shape[0]
    pieces = heads // 8
    groups = 2 * pieces
    wide[...] = query_ref[...].astype(F32)
    levels = spread_levels(part_ref[:, heads].reshape(2 * count, LANES), groups)
    for g in range(groups):
        micro, piece = g // pieces, g % pieces
        rows = slice(piece * 8, (piece + 1) * 8)
        key = key_ref[micro : micro + 1, :].astype(F32)
        own = jnp.sum(wide[rows, micro, :] * key, axis=1, keepdims=True) * scale
        level = levels[g].reshape(count, 8, LANES)
        top = jnp.maximum(jnp.max(level, axis=0), own)
        weight = jnp.exp(level - top[None])
        self_weight = jnp.exp(own - top)
        part = part_ref[:, 4 * g : 4 * (g + 1)].reshape(8 * count, LANES).astype(F32)
        mixed = jnp.sum(weight * part.reshape(count, 8, LANES), axis=0)
        mixed = mixed + self_weight * value_ref[micro : micro + 1, :].astype(F32)
        wide[rows, micro, :] = mixed / (jnp.sum(weight, axis=0) + self_weight)
    out_ref[...] = wide[...].astype(BF16)


def in_hbm(x):
    return pltpu.with_memory_space_constraint(x, pltpu.HBM)


def in_vmem(x):
    return pltpu.with_memory_space_constraint(x, pltpu.VMEM)


def exchange(x, axis):
    return lax.all_to_all(x, axis, 0, 0)


def per_device(
    queries, new_token_keys, new_token_values, key_pool, value_pool, block_list, context_len
):
    planes, tensor = lax.axis_size("zy"), lax.axis_size("tp")
    micros, _, width = queries.shape
    slots, block_len, dim = key_pool.shape
    heads = width // dim
    scale = dim ** (-0.5)
    per = slots // tensor
    swap = [(0, 1), (1, 0)]
    hbm = pl.BlockSpec(memory_space=pltpu.HBM)
    vmem = pl.BlockSpec(memory_space=pltpu.VMEM)
    params = pltpu.CompilerParams(vmem_limit_bytes=32 * 1024 * 1024)
    message = jax.ShapeDtypeStruct((planes, heads + 1, micros, LANES), BF16)
    query = queries.reshape(micros, heads, dim).transpose(1, 0, 2)

    with jax.named_scope("queries_to_holders"):
        listed, lengths = block_list.transpose(0, 2, 1), context_len.transpose(1, 0)
        packed = pl.pallas_call(
            functools.partial(pack_kernel, (slots // micros - 1) * block_len),
            out_shape=message,
            in_specs=[hbm] * 3,
            out_specs=vmem,
            scratch_shapes=[
                pltpu.VMEM(query.shape, BF16),
                pltpu.VMEM(listed.shape, jnp.int32),
                pltpu.VMEM(lengths.shape, jnp.int32),
                pltpu.VMEM(query.shape, F32),
                pltpu.VMEM((8, LANES), F32),
                pltpu.SemaphoreType.DMA((3,)),
            ],
            compiler_params=params,
        )(*(in_hbm(x) for x in (query, listed, lengths)))
        packed, key_pool, value_pool = lax.optimization_barrier((packed, key_pool, value_pool))
        own = exchange(packed, "zy")
        rows = own[:, heads, 0]
        rows = exchange(jnp.broadcast_to(rows[None], (tensor, planes, LANES)), "tp")
    with jax.named_scope("pools_of_both_cores"):
        sib_key = lax.ppermute(key_pool, "c", swap)
        sib_value = lax.ppermute(value_pool, "c", swap)
    with jax.named_scope("block_attention"):
        me = (lax.axis_index("zy") * 2 + lax.axis_index("c")).astype(jnp.int32).reshape(1)
        parts = pl.pallas_call(
            functools.partial(holder_kernel, heads, scale, tensor, per),
            out_shape=message,
            in_specs=[pl.BlockSpec(memory_space=pltpu.SMEM)] + [vmem] * 2 + [hbm] * 2 + [vmem] * 2,
            out_specs=vmem,
            scratch_shapes=[
                pltpu.VMEM(key_pool.shape, BF16),
                pltpu.VMEM(value_pool.shape, BF16),
                pltpu.VMEM((planes + 1, micros * heads, LANES), F32),
                pltpu.VMEM((planes + 1, micros * heads, LANES), F32),
                pltpu.VMEM((planes, 2, LANES), F32),
                pltpu.VMEM((8, LANES), jnp.int32),
                pltpu.SMEM((8, LANES), jnp.int32),
                pltpu.SemaphoreType.DMA((2,)),
                pltpu.SemaphoreType.DMA,
            ],
            compiler_params=params,
        )(me, own, rows, in_hbm(key_pool), in_hbm(value_pool), in_vmem(sib_key), in_vmem(sib_value))
    with jax.named_scope("parts_to_owners"):
        arrived = exchange(parts, "zy")
    with jax.named_scope("owner_sum"):
        out = pl.pallas_call(
            functools.partial(owner_kernel, heads, scale),
            out_shape=jax.ShapeDtypeStruct(query.shape, BF16),
            in_specs=[vmem] * 4,
            out_specs=vmem,
            scratch_shapes=[
                pltpu.VMEM(query.shape, F32),
            ],
            compiler_params=params,
        )(arrived, query, new_token_keys.reshape(micros, dim), new_token_values.reshape(micros, dim))
        return out.transpose(1, 0, 2).reshape(micros, 1, width)


def solution(mesh):
    spread, tensor = mesh.devices.shape
    finer = Mesh(mesh.devices.reshape(spread // 2, 2, tensor), ("zy", "c", "tp"))
    dp = ("zy", "c")
    placed = (
        P(None, dp, "tp"),
        P(None, dp, "tp"),
        P(None, dp, "tp"),
        P(dp, None, "tp"),
        P(dp, None, "tp"),
        P(None, ("zy", "c", "tp"), None),
        P(None, dp),
    )
    return jax.shard_map(
        per_device, mesh=finer, in_specs=placed, out_specs=P(None, dp, "tp"), check_vma=False
    )
```

time: 91.3 us -> 85.9 us (0.941)
  waiting for transfers between devices: 7.38 us -> 5.63 us
  blocking collectives: 61.7 us -> 60 us
  other arithmetic: 1.34 us -> 0 us
    ppermute x2, waiting for transfers between devices: 1.83 us -> 0.01 us  [the longest x1 0.01 us: per_device(): sib_key = lax.ppermute(key_pool, 'c', swap)]
    all_to_all x2, blocking collectives: 61.7 us -> 60 us  [exchange(): return lax.all_to_all(x, axis, 0, 0)]
    pallas_call x2 -> x1, Pallas kernels: 2.61 us -> 1.04 us  [per_device(): pl.pallas_call(functools.partial(pack_kernel, (slots // micros - 1) * blo...]
    pallas_call x1, Pallas kernels: 6.41 us -> 7.98 us  [per_device(): pl.pallas_call(functools.partial(holder_kernel, heads, scale, tensor, per...]
  transfers between devices with their start and end apart: 3 -> 3, of which waited for: 2 -> 1; matrix products, arithmetic and copies ran while one was open for 1% -> 1% of each run, Pallas kernels for 0% -> 0%
where the time goes in v4:
time: 85.9 us; the launch traced here: 85.5 us
  blocking collectives  60 us (70%)
  Pallas kernels  10.5 us (12%)
  starting transfers between devices  8.62 us (10%)
  waiting for transfers between devices  5.63 us (7%)
    all_to_all x2, blocking collectives, exchange(): return lax.all_to_all(x, axis, 0, 0)  60 us
    pallas_call x1, Pallas kernels, per_device(): pl.pallas_call(functools.partial(holder_kernel, heads, scale, tensor, per...  7.98 us
    all_to_all x1, waiting for transfers between devices, exchange(): return lax.all_to_all(x, axis, 0, 0)  5.63 us
    all_to_all x1, starting transfers between devices, exchange(): return lax.all_to_all(x, axis, 0, 0)  4.29 us
    ppermute x1, starting transfers between devices, per_device(): sib_value = lax.ppermute(value_pool, 'c', swap)  2.41 us
    ppermute x1, starting transfers between devices, per_device(): sib_key = lax.ppermute(key_pool, 'c', swap)  1.92 us
  transfers between devices with their start and end apart: 3, of which 1 were waited for; matrix products, arithmetic and copies ran while one was open for 1% of the time, Pallas kernels for 0%

profile of v4, /device:TPU:8, one launch (start us, length us, event | category | flops | bytes accessed | tf_op | source)
XLA Modules:
  0.0 85.5 jit_solution(5533916137561800682)
XLA Ops:
  0.0 1.0 %queries_to_holders.1 = bf16[64,17,2,128]{3,2,1,0:T(2,128)(2,1)S(1)} custom-call(bf16[16,2,128]{2,1,0:T(2,128)(2,1)} %bitcast.14, s32[2,2,8]{2,1,0:T(2,128)} %bitcast.19, s32[1,2]{1,0:T(1,128)} %bitcast.20), custom_call_target="tpu_custom_call" | custom-call | tf_op jit(solution)/shard_map/queries_to_holders/pallas_call | solution.py:276
  1.0 1.9 %collective-permute-start = (bf16[64,128,128]{2,1,0:T(8,128)(2,1)}, bf16[64,128,128]{2,1,0:T(8,128)(2,1)S(1)}, u32[]{:S(2)}, u32[]{:S(2)}) collective-permute-start(bf16[64,128,128]{2,1,0:T(8,128)(2,1)} %key_ref), channel_id=1, source_target_pairs={{0,4},{4,0},{1,5},{5,1},{2,6},{6,2},{3,7},{7,3},{8,12},{12,8},{9,1... | collective-permute-start | bytes 6291464 | tf_op jit(solution)/shard_map/pools_of_both_cores/ppermute | solution.py:296
  3.0 2.4 %collective-permute-start.1 = (bf16[64,128,128]{2,1,0:T(8,128)(2,1)}, bf16[64,128,128]{2,1,0:T(8,128)(2,1)}, u32[]{:S(2)}, u32[]{:S(2)}) collective-permute-start(bf16[64,128,128]{2,1,0:T(8,128)(2,1)} %value_ref), channel_id=1, source_target_pairs={{0,4},{4,0},{1,5},{5,1},{2,6},{6,2},{3,7},{7,3},{8,12},{12,8},{9,1... | collective-permute-start | bytes 6291464 | tf_op jit(solution)/shard_map/pools_of_both_cores/ppermute | solution.py:297
  5.4 36.4 %all_to_all.15.own_ref = bf16[64,17,2,128]{3,2,1,0:T(2,128)(2,1)S(1)} all-to-all(bf16[64,17,2,128]{3,2,1,0:T(2,128)(2,1)S(1)} %queries_to_holders.1), channel_id=1, replica_groups=mesh['zy'=64,'c'=2,'tp'=4] {'zy'}, dimensions={0} | all-to-all | bytes 1114112 | tf_op jit(solution)/shard_map/queries_to_holders/all_to_all | solution.py:255
  41.9 0.6 broadcast_in_dim.8
  42.5 4.3 %all-to-all-start.1 = ((bf16[4,64,128]{2,1,0:T(8,128)(2,1)}), bf16[4,64,128]{2,1,0:T(8,128)(2,1)S(1)}, u32[]{:S(2)}, u32[]{:S(2)}) async-start(bf16[4,64,128]{2,1,0:T(8,128)(2,1)} %broadcast_in_dim.8), calls=%async_computation.1 | async-start | bytes 131072 | tf_op jit(solution)/shard_map/queries_to_holders/all_to_all | solution.py:255
  46.8 5.6 %all-to-all-done.1.entry_ref = bf16[4,64,128]{2,1,0:T(8,128)(2,1)S(1)} async-done(((bf16[4,64,128]{2,1,0:T(8,128)(2,1)}), bf16[4,64,128]{2,1,0:T(8,128)(2,1)S(1)}, u32[]{:S(2)}, u32[]{:S(2)}) %all-to-all-start.1) | async-done | bytes 65568 | tf_op jit(solution)/shard_map/queries_to_holders/all_to_all | solution.py:255
  52.4 0.0 collective-permute-done.sib_key_ref
  52.4 0.0 collective-permute-done.1.sib_value_ref
  52.4 0.0 copy-start
  52.4 0.0 copy-start.1
  52.4 0.0 copy-start.2
  52.4 8.0 %block_attention.1 = bf16[64,17,2,128]{3,2,1,0:T(2,128)(2,1)S(1)} custom-call(s32[1]{0:T(128)} %bitcast.me, bf16[64,17,2,128]{3,2,1,0:T(2,128)(2,1)S(1)} %all_to_all.15.own_ref, bf16[4,64,128]{2,1,0:T(8,128)(2,1)S(1)} %all-to-all-done.1.entry_ref, bf16[64,128,128]{2,1,0:T(8,128)(2,1)} %key_ref, bf16[64,128,128]{2,1,0:T(8,128)(2,1)} %value_ref, ...), custom_call_target="tpu_custom_call" | custom-call | tf_op jit(solution)/shard_map/block_attention/pallas_call | solution.py:300
  60.4 23.6 %all_to_all.16.part_ref = bf16[64,17,2,128]{3,2,1,0:T(2,128)(2,1)S(1)} all-to-all(bf16[64,17,2,128]{3,2,1,0:T(2,128)(2,1)S(1)} %block_attention.1), channel_id=1, replica_groups=mesh['zy'=64,'c'=2,'tp'=4] {'zy'}, dimensions={0} | all-to-all | bytes 1114112 | tf_op jit(solution)/shard_map/parts_to_owners/all_to_all | solution.py:255
  84.0 0.0 copy-done
  84.0 0.0 copy-done.1
  84.0 0.0 copy-done.2
  84.0 1.5 %owner_sum.1 = bf16[16,2,128]{2,1,0:T(2,128)(2,1)} custom-call(bf16[64,17,2,128]{3,2,1,0:T(2,128)(2,1)S(1)} %all_to_all.16.part_ref, bf16[16,2,128]{2,1,0:T(2,128)(2,1)S(1)} %bitcast.15, bf16[2,128]{1,0:T(2,128)(2,1)S(1)} %bitcast.16, bf16[2,128]{1,0:T(2,128)(2,1)S(1)} %bitcast.17), custom_call_target="tpu_custom_call" | custom-call | tf_op jit(solution)/shard_map/owner_sum/pallas_call | solution.py:321
  (2 shorter events, 0.0 us)
Async XLA Ops:
  1.0 51.4 %collective-permute-start = (bf16[64,128,128]{2,1,0:T(8,128)(2,1)}, bf16[64,128,128]{2,1,0:T(8,128)(2,1)S(1)}, u32[]{:S(2)}, u32[]{:S(2)}) collective-permute-start(bf16[64,128,128]{2,1,0:T(8,128)(2,1)} %key_ref), channel_id=1, source_target_pairs={{0,4},{4,0},{1,5},{5,1},{2,6},{6,2},{3,7},{7,3},{8,12},{12,8},{9,1... | collective-permute-start | bytes 6291464 | tf_op jit(solution)/shard_map/pools_of_both_cores/ppermute | solution.py:296
  3.0 49.4 %collective-permute-start.1 = (bf16[64,128,128]{2,1,0:T(8,128)(2,1)}, bf16[64,128,128]{2,1,0:T(8,128)(2,1)}, u32[]{:S(2)}, u32[]{:S(2)}) collective-permute-start(bf16[64,128,128]{2,1,0:T(8,128)(2,1)} %value_ref), channel_id=1, source_target_pairs={{0,4},{4,0},{1,5},{5,1},{2,6},{6,2},{3,7},{7,3},{8,12},{12,8},{9,1... | collective-permute-start | bytes 6291464 | tf_op jit(solution)/shard_map/pools_of_both_cores/ppermute | solution.py:297
  42.5 9.9 %all-to-all-start.1 = ((bf16[4,64,128]{2,1,0:T(8,128)(2,1)}), bf16[4,64,128]{2,1,0:T(8,128)(2,1)S(1)}, u32[]{:S(2)}, u32[]{:S(2)}) async-start(bf16[4,64,128]{2,1,0:T(8,128)(2,1)} %broadcast_in_dim.8), calls=%async_computation.1 | async-start | bytes 131072 | tf_op jit(solution)/shard_map/queries_to_holders/all_to_all | solution.py:255
  52.4 31.6 %copy-start = (bf16[2,1,2048]{2,0,1:T(2,128)(2,1)S(1)}, bf16[2,1,2048]{2,0,1:T(2,128)(2,1)}, u32[]{:S(2)}) copy-start(bf16[2,1,2048]{2,0,1:T(2,128)(2,1)} %param.7) | copy-start | bytes 24580
  52.4 31.6 %copy-start.1 = (bf16[2,1,128]{2,0,1:T(2,128)(2,1)S(1)}, bf16[2,1,128]{2,0,1:T(2,128)(2,1)}, u32[]{:S(2)}) copy-start(bf16[2,1,128]{2,0,1:T(2,128)(2,1)} %param.8) | copy-start | bytes 1540
  52.4 31.6 %copy-start.2 = (bf16[2,1,128]{2,0,1:T(2,128)(2,1)S(1)}, bf16[2,1,128]{2,0,1:T(2,128)(2,1)}, u32[]{:S(2)}) copy-start(bf16[2,1,128]{2,0,1:T(2,128)(2,1)} %param.9) | copy-start | bytes 1540

commit v5 on v4

--- a/solution.py
+++ b/solution.py
@@ -8,6 +8,7 @@
 from jax.sharding import Mesh, PartitionSpec as P
 
 LANES = 128
+COST = 10**11
 FIELD = 16
 SPAN = 32
 EMPTY = -1e30
@@ -41,64 +42,55 @@
     return [levels[:, g * LANES : (g + 1) * LANES] for g in range(groups)]
 
 
-def pack_kernel(
-    first_tail, query_hbm, list_hbm, length_hbm, out_ref, query_ref, list_ref, length_ref,
-    wide, rows, sems,
+def first_kernel(
+    first_tail, query_hbm, list_hbm, length_hbm, copies_ref, query_ref, tail_ref,
+    narrow, entries, lengths, wide, rows, sems,
 ):
-    heads, micros, _ = query_ref.shape
-    per = list_ref.shape[2]
+    heads, micros, _ = narrow.shape
     loads = [
-        pltpu.make_async_copy(query_hbm, query_ref, sems.at[0]),
-        pltpu.make_async_copy(list_hbm, list_ref, sems.at[1]),
-        pltpu.make_async_copy(length_hbm, length_ref, sems.at[2]),
+        pltpu.make_async_copy(list_hbm, entries, sems.at[0]),
+        pltpu.make_async_copy(query_hbm, narrow, sems.at[1]),
+        pltpu.make_async_copy(length_hbm, lengths, sems.at[2]),
     ]
     for load in loads:
         load.start()
     rows[...] = jnp.zeros(rows.shape, F32)
-    for load in loads:
-        load.wait()
-    wide[...] = query_ref[...].astype(F32)
+    loads[0].wait()
+    copies_ref[...] = jnp.broadcast_to(entries[...][None], copies_ref.shape)
+    loads[1].wait()
+    wide[...] = narrow[...].astype(F32)
     query = jnp.concatenate([wide[:, m, :] for m in range(micros)], axis=0).astype(BF16)
-    for m in range(micros):
-        rows[2 * m : 2 * m + 2, :per] = list_ref[m].astype(F32)
-    rows[2 * micros : 2 * micros + 1, :micros] = (length_ref[...] - first_tail).astype(F32)
-    row = pltpu.roll(rows[2 * micros : 2 * micros + 1, :], 2 * FIELD, 1)
-    for m in range(micros):
-        for field in range(2):
-            at = 2 * m + field
-            shift = field * FIELD + m * per
-            entry = rows[at : at + 1, :]
-            row = row + (pltpu.roll(entry, shift, 1) if shift else entry)
-    listed = jnp.concatenate([row, jnp.zeros((1, LANES), F32)], axis=0).astype(BF16)
-    message = jnp.concatenate([query.reshape(heads, micros, LANES), listed[None]], axis=0)
+    query_ref[...] = query.reshape(heads, micros, LANES)
+    loads[2].wait()
+    rows[0:1, :micros] = (lengths[...] - first_tail).astype(F32)
+    tail_ref[...] = rows[...]
+
+
+def pack_kernel(query_ref, list_ref, tail_ref, out_ref, rows):
+    tensor, micros, _, part = list_ref.shape
+    rows[...] = jnp.zeros(rows.shape, F32)
+    fields = []
+    for t in range(tensor):
+        for m in range(micros):
+            at = 2 * (t * micros + m)
+            rows[at : at + 2, :part] = list_ref[t, m].astype(F32)
+            fields.extend((at + field, t * SPAN + field * FIELD + m * part) for field in range(2))
+    entries = rows[0:1, :]
+    for line, shift in fields[1:]:
+        entries = entries + pltpu.roll(rows[line : line + 1, :], shift, 1)
+    listed = jnp.concatenate([entries, tail_ref[0:1, :]], axis=0).astype(BF16)
+    message = jnp.concatenate([query_ref[...], listed[None]], axis=0)
     out_ref[...] = jnp.broadcast_to(message[None], out_ref.shape)
 
 
-def holder_kernel(
-    heads, scale, tensor, per, me, own_ref, entry_ref, key_ref, value_ref, sib_key_ref,
-    sib_value_ref, out_ref, keys, values, mixed, levels, pad, found, spots, sems, spot_sem,
-):
-    ranks = own_ref.shape[0]
-    slots, block_len, _ = keys.shape
-    entries = slots
+def find_kernel(tensor, per, me, own_ref, found_ref, pad):
+    ranks, heads = own_ref.shape[0], own_ref.shape[1] - 1
+    entries = tensor * per
     per_micro = entries // 2
-    groups = 2 * heads // 8
-    loads = [
-        pltpu.make_async_copy(key_ref, keys, sems.at[0]),
-        pltpu.make_async_copy(value_ref, values, sems.at[1]),
-    ]
-    for load in loads:
-        load.start()
-    pools = ((sib_key_ref, sib_value_ref), (keys, values))
-
     lane = lane_ids((ranks, LANES))
-    listed = jnp.zeros((ranks, LANES), F32)
-    for t in range(tensor):
-        quarter = entry_ref[t].astype(F32)
-        if t == 0:
-            tails = quarter
-        moved = pltpu.roll(quarter, t * SPAN, 1) if t else quarter
-        listed = jnp.where(lane // SPAN == t, moved, listed)
+    pad[...] = own_ref[:, heads].astype(F32)
+    listed = pad[:, 0, :]
+    tails = pad[:, 1, :]
     index = lane % FIELD
     order = (index // (per // 2)) * per_micro + (lane // SPAN) * (per // 2) + index % (per // 2)
     place = (lane % SPAN < per) & (lane < tensor * SPAN)
@@ -122,8 +114,8 @@
     )
     chosen = valid & (before == (lane % (LANES // 2)).astype(F32))
     rank = lax.broadcasted_iota(jnp.int32, (ranks, LANES), 0).astype(F32)
-    tail0 = jnp.sum(jnp.where(lane == 2 * FIELD, tails, 0.0), axis=1, keepdims=True)
-    tail1 = jnp.sum(jnp.where(lane == 2 * FIELD + 1, tails, 0.0), axis=1, keepdims=True)
+    tail0 = jnp.sum(jnp.where(lane == 0, tails, 0.0), axis=1, keepdims=True)
+    tail1 = jnp.sum(jnp.where(lane == 1, tails, 0.0), axis=1, keepdims=True)
 
     def listing(x):
         return jnp.sum(jnp.where(chosen, x, 0.0), axis=0, keepdims=True)
@@ -132,15 +124,38 @@
     lines[0] = jnp.where(listing(1.0) > 0.0, lines[0], float(ranks))
     lines.append(jnp.sum(valid.astype(F32), axis=0, keepdims=True))
     lines.append(jnp.zeros((8 - len(lines), LANES), F32))
-    found[...] = jnp.concatenate(lines, axis=0).astype(jnp.int32)
-    move = pltpu.make_async_copy(found, spots, spot_sem)
+    found_ref[...] = jnp.concatenate(lines, axis=0).astype(jnp.int32)
+
+
+def holder_kernel(
+    heads, scale, own_ref, found_ref, key_ref, value_ref, sib_key_ref, sib_value_ref,
+    out_ref, keys, values, mixed, levels, tiles, pad, spots, sems, spot_sem,
+):
+    ranks = own_ref.shape[0]
+    slots, block_len, _ = keys.shape
+    entries = slots
+    per_micro = entries // 2
+    groups = 2 * heads // 8
+    move = pltpu.make_async_copy(found_ref, spots, spot_sem)
     move.start()
+    loads = [
+        pltpu.make_async_copy(key_ref, keys, sems.at[0]),
+        pltpu.make_async_copy(value_ref, values, sems.at[1]),
+    ]
+    for load in loads:
+        load.start()
+    pools = ((sib_key_ref, sib_value_ref), (keys, values))
     mixed[...] = jnp.zeros(mixed.shape, F32)
     levels[...] = jnp.full(levels.shape, EMPTY, F32)
     pad[...] = jnp.zeros(pad.shape, F32)
+    lane8 = lane_ids((8, LANES))
+    sublane = lax.broadcasted_iota(jnp.int32, (8, LANES), 0)
+    field = jnp.where(lane8 // FIELD == sublane, lane8 % FIELD, FIELD)
+    blank = jnp.where(field < PARTS * groups, EMPTY, 0.0)
+    tiles[...] = jnp.broadcast_to(blank[None], tiles.shape)
     move.wait()
 
-    together = min(4, slots // 2)
+    together = min(8, slots // 2)
     token = lane_ids((heads, block_len))
 
     def step(pool, i, carry):
@@ -179,12 +194,13 @@
                 preferred_element_type=F32,
             )
             outs.append(part * share[k * heads : (k + 1) * heads])
-        news = []
+        news, made = [], []
         for k in range(together):
             micro_a, micro_b = work[2 * k][2], work[2 * k + 1][2]
             level_a = level[2 * k * heads : (2 * k + 1) * heads]
             level_b = level[(2 * k + 1) * heads : (2 * k + 2) * heads]
             old_mixed, old_level = olds[k]
+            tile = jnp.zeros((8, LANES), F32)
             for micro in range(2):
                 rows = slice(micro * heads, (micro + 1) * heads)
                 la = jnp.where(micro_a == micro, level_a, EMPTY)
@@ -195,10 +211,18 @@
                 wb = jnp.exp(lb - top) * (micro_b == micro).astype(F32)
                 both = wo + wa + wb
                 part = wo * old_mixed[rows] + wa * outs[2 * k] + wb * outs[2 * k + 1]
-                news.append((work[2 * k][0], rows, part / both, top + jnp.log(both)))
+                depth = top + jnp.log(both)
+                news.append((work[2 * k][0], rows, part / both, depth))
+                for piece in range(heads // 8):
+                    group = micro * (heads // 8) + piece
+                    for j, term in enumerate(split3(depth[piece * 8 : (piece + 1) * 8])):
+                        tile = jnp.where(field == PARTS * group + j, term, tile)
+            made.append((work[2 * k][0], tile))
         for where, rows, part, depth in news:
             mixed[where, rows] = part
             levels[where, rows] = depth
+        for where, tile in made:
+            tiles[where] = tile
         return carry
 
     for pool in range(2):
@@ -209,14 +233,7 @@
         steps = (count + together - 1) // together
         lax.fori_loop(0, steps, functools.partial(step, pool), 0)
 
-    sublane = lax.broadcasted_iota(jnp.int32, (1, 8, LANES), 1)
-    lane8 = lane_ids((1, 8, LANES))
-    field = jnp.where(lane8 // FIELD == sublane, lane8 % FIELD, FIELD)
-    tile = jnp.zeros((ranks, 8, LANES), F32)
-    for g in range(groups):
-        for j, term in enumerate(split3(levels[:ranks, 8 * g : 8 * (g + 1)])):
-            tile = jnp.where(field == PARTS * g + j, term, tile)
-    pad[:, 0, :] = jnp.sum(tile, axis=1)
+    pad[:, 0, :] = jnp.sum(tiles[:ranks], axis=1)
     out_ref[:, heads] = pad[...].astype(BF16)
     out_ref[:, :heads] = mixed[:ranks].astype(BF16).reshape(ranks, heads, 2, LANES)
 
@@ -273,11 +290,15 @@
 
     with jax.named_scope("queries_to_holders"):
         listed, lengths = block_list.transpose(0, 2, 1), context_len.transpose(1, 0)
-        packed = pl.pallas_call(
-            functools.partial(pack_kernel, (slots // micros - 1) * block_len),
-            out_shape=message,
+        copies, ordered, tails = pl.pallas_call(
+            functools.partial(first_kernel, (slots // micros - 1) * block_len),
+            out_shape=(
+                jax.ShapeDtypeStruct((tensor, *listed.shape), jnp.int32),
+                jax.ShapeDtypeStruct(query.shape, BF16),
+                jax.ShapeDtypeStruct((8, LANES), F32),
+            ),
             in_specs=[hbm] * 3,
-            out_specs=vmem,
+            out_specs=(vmem,) * 3,
             scratch_shapes=[
                 pltpu.VMEM(query.shape, BF16),
                 pltpu.VMEM(listed.shape, jnp.int32),
@@ -287,34 +308,50 @@
                 pltpu.SemaphoreType.DMA((3,)),
             ],
             compiler_params=params,
-        )(*(in_hbm(x) for x in (query, listed, lengths)))
-        packed, key_pool, value_pool = lax.optimization_barrier((packed, key_pool, value_pool))
+        )(in_hbm(query), in_hbm(listed), in_hbm(lengths))
+        packed = pl.pallas_call(
+            pack_kernel,
+            out_shape=message,
+            in_specs=[vmem] * 3,
+            out_specs=vmem,
+            scratch_shapes=[pltpu.VMEM((2 * tensor * micros, LANES), F32)],
+            compiler_params=params,
+        )(ordered, exchange(copies, "tp"), tails)
         own = exchange(packed, "zy")
-        rows = own[:, heads, 0]
-        rows = exchange(jnp.broadcast_to(rows[None], (tensor, planes, LANES)), "tp")
     with jax.named_scope("pools_of_both_cores"):
         sib_key = lax.ppermute(key_pool, "c", swap)
         sib_value = lax.ppermute(value_pool, "c", swap)
     with jax.named_scope("block_attention"):
         me = (lax.axis_index("zy") * 2 + lax.axis_index("c")).astype(jnp.int32).reshape(1)
+        found = pl.pallas_call(
+            functools.partial(find_kernel, tensor, per),
+            out_shape=jax.ShapeDtypeStruct((8, LANES), jnp.int32),
+            in_specs=[pl.BlockSpec(memory_space=pltpu.SMEM), vmem],
+            out_specs=vmem,
+            scratch_shapes=[pltpu.VMEM((planes, 2, LANES), F32)],
+            compiler_params=params,
+            cost_estimate=pl.CostEstimate(
+                flops=COST, bytes_accessed=2 * own.size, transcendentals=0
+            ),
+        )(me, own)
         parts = pl.pallas_call(
-            functools.partial(holder_kernel, heads, scale, tensor, per),
+            functools.partial(holder_kernel, heads, scale),
             out_shape=message,
-            in_specs=[pl.BlockSpec(memory_space=pltpu.SMEM)] + [vmem] * 2 + [hbm] * 2 + [vmem] * 2,
+            in_specs=[vmem] * 2 + [hbm] * 2 + [vmem] * 2,
             out_specs=vmem,
             scratch_shapes=[
                 pltpu.VMEM(key_pool.shape, BF16),
                 pltpu.VMEM(value_pool.shape, BF16),
                 pltpu.VMEM((planes + 1, micros * heads, LANES), F32),
                 pltpu.VMEM((planes + 1, micros * heads, LANES), F32),
+                pltpu.VMEM((planes + 1, 8, LANES), F32),
                 pltpu.VMEM((planes, 2, LANES), F32),
-                pltpu.VMEM((8, LANES), jnp.int32),
                 pltpu.SMEM((8, LANES), jnp.int32),
                 pltpu.SemaphoreType.DMA((2,)),
                 pltpu.SemaphoreType.DMA,
             ],
             compiler_params=params,
-        )(me, own, rows, in_hbm(key_pool), in_hbm(value_pool), in_vmem(sib_key), in_vmem(sib_value))
+        )(own, found, in_hbm(key_pool), in_hbm(value_pool), in_vmem(sib_key), in_vmem(sib_value))
     with jax.named_scope("parts_to_owners"):
         arrived = exchange(parts, "zy")
     with jax.named_scope("owner_sum"):

time: 85.9 us -> 78.9 us (0.919)
  blocking collectives: 60 us -> 33.1 us
  starting transfers between devices: 8.62 us -> 20.9 us
  waiting for transfers between devices: 5.63 us -> 14.3 us
    all_to_all x2, blocking collectives: 60 us -> 33.1 us  [exchange(): return lax.all_to_all(x, axis, 0, 0)]
    all_to_all x1, starting transfers between devices: 4.29 us -> 16.6 us  [exchange(): return lax.all_to_all(x, axis, 0, 0)]
    all_to_all x1, waiting for transfers between devices: 5.63 us -> 14.3 us  [exchange(): return lax.all_to_all(x, axis, 0, 0)]
    pallas_call x2 -> x4, Pallas kernels: 9.02 us -> 8.57 us  [the longest x1 6.33 us: per_device(): pl.pallas_call(functools.partial(holder_kernel, heads, scale), out_shape=...]
  transfers between devices with their start and end apart: 3 -> 3, of which waited for: 1 -> 1; matrix products, arithmetic and copies ran while one was open for 1% -> 0% of each run, Pallas kernels for 0% -> 0%
where the time goes in v5:
time: 78.9 us; the launch traced here: 78.5 us
  blocking collectives  33.1 us (42%)
  starting transfers between devices  20.9 us (26%)
  waiting for transfers between devices  14.3 us (18%)
  Pallas kernels  10 us (13%)
    all_to_all x2, blocking collectives, exchange(): return lax.all_to_all(x, axis, 0, 0)  33.1 us
    all_to_all x1, starting transfers between devices, exchange(): return lax.all_to_all(x, axis, 0, 0)  16.6 us
    all_to_all x1, waiting for transfers between devices, exchange(): return lax.all_to_all(x, axis, 0, 0)  14.3 us
    pallas_call x1, Pallas kernels, per_device(): pl.pallas_call(functools.partial(holder_kernel, heads, scale), out_shape=...  6.33 us
    ppermute x1, starting transfers between devices, per_device(): sib_value = lax.ppermute(value_pool, 'c', swap)  2.41 us
    ppermute x1, starting transfers between devices, per_device(): sib_key = lax.ppermute(key_pool, 'c', swap)  1.92 us
  transfers between devices with their start and end apart: 3, of which 1 were waited for; matrix products, arithmetic and copies ran while one was open for 0% of the time, Pallas kernels for 0%

profile of v5, /device:TPU:8, one launch (start us, length us, event | category | flops | bytes accessed | tf_op | source)
XLA Modules:
  0.0 78.5 jit_solution(2443060895961281569)
XLA Ops:
  0.0 0.8 queries_to_holders.2
  0.8 9.4 %all_to_all.15.list_ref = s32[4,2,2,8]{3,2,1,0:T(2,128)S(1)} all-to-all(s32[4,2,2,8]{3,2,1,0:T(2,128)S(1)} %get-tuple-element.9), channel_id=1, replica_groups=mesh['zy'=64,'c'=2,'tp'=4] {'tp'}, dimensions={0} | all-to-all | bytes 1024 | tf_op jit(solution)/shard_map/queries_to_holders/all_to_all | solution.py:272
  10.2 1.1 %queries_to_holders.3 = bf16[64,17,2,128]{3,2,1,0:T(2,128)(2,1)} custom-call(bf16[16,2,128]{2,1,0:T(2,128)(2,1)S(1)} %get-tuple-element.8.query_ref, s32[4,2,2,8]{3,2,1,0:T(2,128)S(1)} %all_to_all.15.list_ref, f32[8,128]{1,0:T(8,128)S(1)} %get-tuple-element.10.tail_ref), custom_call_target="tpu_custom_call" | custom-call | tf_op jit(solution)/shard_map/queries_to_holders/pallas_call | solution.py:312
  11.3 16.6 %all-to-all-start.1 = ((bf16[64,17,2,128]{3,2,1,0:T(2,128)(2,1)}), bf16[64,17,2,128]{3,2,1,0:T(2,128)(2,1)S(1)}, u32[]{:S(2)}, u32[]{:S(2)}) async-start(bf16[64,17,2,128]{3,2,1,0:T(2,128)(2,1)} %queries_to_holders.3), calls=%async_computation.1 | async-start | bytes 1114112 | tf_op jit(solution)/shard_map/queries_to_holders/all_to_all | solution.py:272
  27.9 1.9 %collective-permute-start = (bf16[64,128,128]{2,1,0:T(8,128)(2,1)}, bf16[64,128,128]{2,1,0:T(8,128)(2,1)S(1)}, u32[]{:S(2)}, u32[]{:S(2)}) collective-permute-start(bf16[64,128,128]{2,1,0:T(8,128)(2,1)} %key_ref.1), channel_id=1, source_target_pairs={{0,4},{4,0},{1,5},{5,1},{2,6},{6,2},{3,7},{7,3},{8,12},{12,8},{9,1... | collective-permute-start | bytes 6291464 | tf_op jit(solution)/shard_map/pools_of_both_cores/ppermute | solution.py:322
  29.8 2.4 %collective-permute-start.1 = (bf16[64,128,128]{2,1,0:T(8,128)(2,1)}, bf16[64,128,128]{2,1,0:T(8,128)(2,1)}, u32[]{:S(2)}, u32[]{:S(2)}) collective-permute-start(bf16[64,128,128]{2,1,0:T(8,128)(2,1)} %value_ref.1), channel_id=1, source_target_pairs={{0,4},{4,0},{1,5},{5,1},{2,6},{6,2},{3,7},{7,3},{8,12},{12,8},{9,1... | collective-permute-start | bytes 6291464 | tf_op jit(solution)/shard_map/pools_of_both_cores/ppermute | solution.py:323
  32.3 14.3 %all-to-all-done.1.own_ref = bf16[64,17,2,128]{3,2,1,0:T(2,128)(2,1)S(1)} async-done(((bf16[64,17,2,128]{3,2,1,0:T(2,128)(2,1)}), bf16[64,17,2,128]{3,2,1,0:T(2,128)(2,1)S(1)}, u32[]{:S(2)}, u32[]{:S(2)}) %all-to-all-start.1) | async-done | bytes 557088 | tf_op jit(solution)/shard_map/queries_to_holders/all_to_all | solution.py:272
  46.6 0.4 block_attention.2.found_ref
  46.9 0.0 copy-start
  46.9 0.0 copy-start.1
  47.0 0.0 copy-start.2
  47.0 0.0 collective-permute-done.sib_key_ref
  47.0 0.0 collective-permute-done.1.sib_value_ref
  47.0 6.3 %block_attention.3 = bf16[64,17,2,128]{3,2,1,0:T(2,128)(2,1)S(1)} custom-call(bf16[64,17,2,128]{3,2,1,0:T(2,128)(2,1)S(1)} %all-to-all-done.1.own_ref, s32[8,128]{1,0:T(8,128)S(1)} %block_attention.2.found_ref, bf16[64,128,128]{2,1,0:T(8,128)(2,1)} %key_ref.1, bf16[64,128,128]{2,1,0:T(8,128)(2,1)} %value_ref.1, ...), custom_call_target="tpu_custom_call" | custom-call | tf_op jit(solution)/shard_map/block_attention/pallas_call | solution.py:337
  53.3 23.7 %all_to_all.16.part_ref = bf16[64,17,2,128]{3,2,1,0:T(2,128)(2,1)S(1)} all-to-all(bf16[64,17,2,128]{3,2,1,0:T(2,128)(2,1)S(1)} %block_attention.3), channel_id=1, replica_groups=mesh['zy'=64,'c'=2,'tp'=4] {'zy'}, dimensions={0} | all-to-all | bytes 1114112 | tf_op jit(solution)/shard_map/parts_to_owners/all_to_all | solution.py:272
  77.0 0.0 copy-done
  77.0 0.0 copy-done.1
  77.0 0.0 copy-done.2
  77.0 1.5 %owner_sum.1 = bf16[16,2,128]{2,1,0:T(2,128)(2,1)} custom-call(bf16[64,17,2,128]{3,2,1,0:T(2,128)(2,1)S(1)} %all_to_all.16.part_ref, bf16[16,2,128]{2,1,0:T(2,128)(2,1)S(1)} %bitcast.12, bf16[2,128]{1,0:T(2,128)(2,1)S(1)} %bitcast.13, bf16[2,128]{1,0:T(2,128)(2,1)S(1)} %bitcast.14), custom_call_target="tpu_custom_call" | custom-call | tf_op jit(solution)/shard_map/owner_sum/pallas_call | solution.py:358
Async XLA Ops:
  11.3 35.3 %all-to-all-start.1 = ((bf16[64,17,2,128]{3,2,1,0:T(2,128)(2,1)}), bf16[64,17,2,128]{3,2,1,0:T(2,128)(2,1)S(1)}, u32[]{:S(2)}, u32[]{:S(2)}) async-start(bf16[64,17,2,128]{3,2,1,0:T(2,128)(2,1)} %queries_to_holders.3), calls=%async_computation.1 | async-start | bytes 1114112 | tf_op jit(solution)/shard_map/queries_to_holders/all_to_all | solution.py:272
  27.9 19.1 %collective-permute-start = (bf16[64,128,128]{2,1,0:T(8,128)(2,1)}, bf16[64,128,128]{2,1,0:T(8,128)(2,1)S(1)}, u32[]{:S(2)}, u32[]{:S(2)}) collective-permute-start(bf16[64,128,128]{2,1,0:T(8,128)(2,1)} %key_ref.1), channel_id=1, source_target_pairs={{0,4},{4,0},{1,5},{5,1},{2,6},{6,2},{3,7},{7,3},{8,12},{12,8},{9,1... | collective-permute-start | bytes 6291464 | tf_op jit(solution)/shard_map/pools_of_both_cores/ppermute | solution.py:322
  29.8 17.1 %collective-permute-start.1 = (bf16[64,128,128]{2,1,0:T(8,128)(2,1)}, bf16[64,128,128]{2,1,0:T(8,128)(2,1)}, u32[]{:S(2)}, u32[]{:S(2)}) collective-permute-start(bf16[64,128,128]{2,1,0:T(8,128)(2,1)} %value_ref.1), channel_id=1, source_target_pairs={{0,4},{4,0},{1,5},{5,1},{2,6},{6,2},{3,7},{7,3},{8,12},{12,8},{9,1... | collective-permute-start | bytes 6291464 | tf_op jit(solution)/shard_map/pools_of_both_cores/ppermute | solution.py:323
  46.9 30.1 %copy-start = (bf16[2,1,2048]{2,0,1:T(2,128)(2,1)S(1)}, bf16[2,1,2048]{2,0,1:T(2,128)(2,1)}, u32[]{:S(2)}) copy-start(bf16[2,1,2048]{2,0,1:T(2,128)(2,1)} %param.7) | copy-start | bytes 24580
  46.9 30.1 %copy-start.1 = (bf16[2,1,128]{2,0,1:T(2,128)(2,1)S(1)}, bf16[2,1,128]{2,0,1:T(2,128)(2,1)}, u32[]{:S(2)}) copy-start(bf16[2,1,128]{2,0,1:T(2,128)(2,1)} %param.8) | copy-start | bytes 1540
  47.0 30.1 %copy-start.2 = (bf16[2,1,128]{2,0,1:T(2,128)(2,1)S(1)}, bf16[2,1,128]{2,0,1:T(2,128)(2,1)}, u32[]{:S(2)}) copy-start(bf16[2,1,128]{2,0,1:T(2,128)(2,1)} %param.9) | copy-start | bytes 1540

commit v6 on v5

--- a/solution.py
+++ b/solution.py
@@ -83,7 +83,7 @@
     out_ref[...] = jnp.broadcast_to(message[None], out_ref.shape)
 
 
-def find_kernel(tensor, per, me, own_ref, found_ref, pad):
+def find_kernel(tensor, per, block_len, me, own_ref, found_ref, pad):
     ranks, heads = own_ref.shape[0], own_ref.shape[1] - 1
     entries = tensor * per
     per_micro = entries // 2
@@ -123,18 +123,24 @@
     lines = [listing(x) for x in (rank, first, last, tail0, tail1)]
     lines[0] = jnp.where(listing(1.0) > 0.0, lines[0], float(ranks))
     lines.append(jnp.sum(valid.astype(F32), axis=0, keepdims=True))
-    lines.append(jnp.zeros((8 - len(lines), LANES), F32))
-    found_ref[...] = jnp.concatenate(lines, axis=0).astype(jnp.int32)
+    ranked, code_a, code_b, left0, left1, count = (x.astype(jnp.int32) for x in lines)
+    places, micros, lives = [], [], []
+    for code in (code_a, code_b):
+        at = code % entries
+        micro = at // per_micro
+        left = jnp.where(micro == 0, left0, left1)
+        places.append(code // entries)
+        micros.append(micro)
+        lives.append(jnp.where(at % per_micro == per_micro - 1, left, block_len))
+    found_ref[...] = jnp.concatenate([ranked, *places, *micros, *lives, count], axis=0)
 
 
 def holder_kernel(
     heads, scale, own_ref, found_ref, key_ref, value_ref, sib_key_ref, sib_value_ref,
-    out_ref, keys, values, mixed, levels, tiles, pad, spots, sems, spot_sem,
+    out_ref, keys, values, tops, sums, mixed, parts, tiles, pad, spots, sems, spot_sem,
 ):
     ranks = own_ref.shape[0]
     slots, block_len, _ = keys.shape
-    entries = slots
-    per_micro = entries // 2
     groups = 2 * heads // 8
     move = pltpu.make_async_copy(found_ref, spots, spot_sem)
     move.start()
@@ -145,17 +151,21 @@
     for load in loads:
         load.start()
     pools = ((sib_key_ref, sib_value_ref), (keys, values))
+    tops[...] = jnp.full(tops.shape, EMPTY, F32)
+    sums[...] = jnp.zeros(sums.shape, F32)
     mixed[...] = jnp.zeros(mixed.shape, F32)
-    levels[...] = jnp.full(levels.shape, EMPTY, F32)
+    parts[...] = jnp.zeros(parts.shape, F32)
     pad[...] = jnp.zeros(pad.shape, F32)
     lane8 = lane_ids((8, LANES))
     sublane = lax.broadcasted_iota(jnp.int32, (8, LANES), 0)
     field = jnp.where(lane8 // FIELD == sublane, lane8 % FIELD, FIELD)
-    blank = jnp.where(field < PARTS * groups, EMPTY, 0.0)
-    tiles[...] = jnp.broadcast_to(blank[None], tiles.shape)
+    half = PARTS * groups // 2
+    for micro in range(2):
+        blank = jnp.where((field >= micro * half) & (field < (micro + 1) * half), EMPTY, 0.0)
+        tiles[:, micro] = jnp.broadcast_to(blank[None], (ranks + 1, 8, LANES))
     move.wait()
 
-    together = min(8, slots // 2)
+    together = min(10, slots // 2)
     token = lane_ids((heads, block_len))
 
     def step(pool, i, carry):
@@ -163,79 +173,84 @@
         for k in range(together):
             n = pool * (LANES // 2) + i * together + k
             where = spots[0, n]
-            for line in (1, 2):
-                block = spots[line, n]
-                at = block % entries
-                micro = at // per_micro
-                tail = jnp.where(micro == 0, spots[3, n], spots[4, n])
-                live = jnp.where(at % per_micro == per_micro - 1, tail, block_len)
-                work.append((where, block // entries, micro, live))
-        olds = [(mixed[work[2 * k][0]], levels[work[2 * k][0]]) for k in range(together)]
+            for line in range(2):
+                work.append((where, spots[1 + line, n], spots[3 + line, n], spots[5 + line, n]))
         scores = []
-        for where, block, micro, live in work:
-            inner = pl.ds(micro * (heads // 2), heads // 2)
-            query = own_ref[jnp.minimum(where, ranks - 1), inner].reshape(heads, LANES)
-            score = lax.dot_general(
-                query, pools[pool][0][block], (((1,), (1,)), ((), ())), preferred_element_type=F32
+        for k in range(together):
+            pair = work[2 * k : 2 * k + 2]
+            queries = []
+            for where, block, micro, live in pair:
+                inner = pl.ds(micro * (heads // 2), heads // 2)
+                query = own_ref[jnp.minimum(where, ranks - 1), inner].reshape(heads, LANES)
+                queries.append(query)
+            both = lax.dot_general(
+                jnp.concatenate(queries, axis=0),
+                jnp.concatenate([pools[pool][0][block] for _, block, _, _ in pair], axis=0),
+                (((1,), (1,)), ((), ())),
+                preferred_element_type=F32,
             )
-            scores.append(jnp.where(token < live, score * scale, EMPTY))
+            for line, (where, block, micro, live) in enumerate(pair):
+                score = both[line * heads : (line + 1) * heads, line * block_len : (line + 1) * block_len]
+                scores.append(jnp.where(token < live, score * scale, EMPTY))
         score = jnp.concatenate(scores, axis=0)
         peak = jnp.max(score, axis=1, keepdims=True)
         weight = jnp.exp(score - peak)
         total = jnp.sum(weight, axis=1, keepdims=True)
         weight = weight.astype(BF16)
-        share = 1.0 / total
-        level = peak + jnp.log(total)
-        outs = []
-        for k, (where, block, micro, live) in enumerate(work):
-            part = jnp.dot(
-                weight[k * heads : (k + 1) * heads],
-                pools[pool][1][block],
-                preferred_element_type=F32,
+        nothing = jnp.zeros((heads, block_len), BF16)
+        mixes = []
+        for k in range(together):
+            wa = weight[2 * k * heads : (2 * k + 1) * heads]
+            wb = weight[(2 * k + 1) * heads : (2 * k + 2) * heads]
+            spread = jnp.concatenate(
+                [
+                    jnp.concatenate([wa, nothing], axis=1),
+                    jnp.concatenate([nothing, wb], axis=1),
+                ],
+                axis=0,
             )
-            outs.append(part * share[k * heads : (k + 1) * heads])
-        news, made = [], []
-        for k in range(together):
-            micro_a, micro_b = work[2 * k][2], work[2 * k + 1][2]
-            level_a = level[2 * k * heads : (2 * k + 1) * heads]
-            level_b = level[(2 * k + 1) * heads : (2 * k + 2) * heads]
-            old_mixed, old_level = olds[k]
-            tile = jnp.zeros((8, LANES), F32)
-            for micro in range(2):
-                rows = slice(micro * heads, (micro + 1) * heads)
-                la = jnp.where(micro_a == micro, level_a, EMPTY)
-                lb = jnp.where(micro_b == micro, level_b, EMPTY)
-                top = jnp.maximum(old_level[rows], jnp.maximum(la, lb))
-                wo = jnp.exp(old_level[rows] - top)
-                wa = jnp.exp(la - top) * (micro_a == micro).astype(F32)
-                wb = jnp.exp(lb - top) * (micro_b == micro).astype(F32)
-                both = wo + wa + wb
-                part = wo * old_mixed[rows] + wa * outs[2 * k] + wb * outs[2 * k + 1]
-                depth = top + jnp.log(both)
-                news.append((work[2 * k][0], rows, part / both, depth))
+            pair = jnp.concatenate(
+                [pools[pool][1][work[2 * k][1]], pools[pool][1][work[2 * k + 1][1]]], axis=0
+            )
+            mixes.append(jnp.dot(spread, pair, preferred_element_type=F32))
+        for line in range(2):
+            olds = []
+            for where, block, micro, live in work[line::2]:
+                olds.append((tops[where, micro], sums[where, micro], mixed[where, micro]))
+            news = []
+            for k, (where, block, micro, live) in enumerate(work[line::2]):
+                rows = slice((2 * k + line) * heads, (2 * k + line + 1) * heads)
+                part = mixes[k][line * heads : (line + 1) * heads]
+                old_top, old_sum, old_mixed = olds[k]
+                top = jnp.maximum(old_top, peak[rows])
+                old_scale, scale_here = jnp.exp(old_top - top), jnp.exp(peak[rows] - top)
+                new_sum = old_scale * old_sum + scale_here * total[rows]
+                new_mixed = old_scale * old_mixed + scale_here * part
+                depth = top + jnp.log(new_sum)
+                tile = jnp.zeros((8, LANES), F32)
                 for piece in range(heads // 8):
-                    group = micro * (heads // 8) + piece
                     for j, term in enumerate(split3(depth[piece * 8 : (piece + 1) * 8])):
-                        tile = jnp.where(field == PARTS * group + j, term, tile)
-            made.append((work[2 * k][0], tile))
-        for where, rows, part, depth in news:
-            mixed[where, rows] = part
-            levels[where, rows] = depth
-        for where, tile in made:
-            tiles[where] = tile
+                        tile = jnp.where(field == PARTS * piece + j + micro * half, term, tile)
+                news.append((where, micro, top, new_sum, new_mixed, new_mixed / new_sum, tile))
+            for where, micro, top, new_sum, new_mixed, part, tile in news:
+                tops[where, micro] = top
+                sums[where, micro] = new_sum
+                mixed[where, micro] = new_mixed
+                parts[where, micro] = part
+                tiles[where, micro] = tile
         return carry
 
     for pool in range(2):
         if pool == 1:
             for load in loads:
                 load.wait()
-        count = spots[5, pool * (LANES // 2)]
+        count = spots[7, pool * (LANES // 2)]
         steps = (count + together - 1) // together
         lax.fori_loop(0, steps, functools.partial(step, pool), 0)
 
-    pad[:, 0, :] = jnp.sum(tiles[:ranks], axis=1)
+    pad[:, 0, :] = jnp.sum(tiles[:ranks, 0] + tiles[:ranks, 1], axis=1)
     out_ref[:, heads] = pad[...].astype(BF16)
-    out_ref[:, :heads] = mixed[:ranks].astype(BF16).reshape(ranks, heads, 2, LANES)
+    out_ref[:, :heads] = parts[:ranks].astype(BF16).reshape(ranks, heads, 2, LANES)
 
 
 def owner_kernel(heads, scale, part_ref, query_ref, key_ref, value_ref, out_ref, wide):
@@ -324,7 +339,7 @@
     with jax.named_scope("block_attention"):
         me = (lax.axis_index("zy") * 2 + lax.axis_index("c")).astype(jnp.int32).reshape(1)
         found = pl.pallas_call(
-            functools.partial(find_kernel, tensor, per),
+            functools.partial(find_kernel, tensor, per, block_len),
             out_shape=jax.ShapeDtypeStruct((8, LANES), jnp.int32),
             in_specs=[pl.BlockSpec(memory_space=pltpu.SMEM), vmem],
             out_specs=vmem,
@@ -342,9 +357,8 @@
             scratch_shapes=[
                 pltpu.VMEM(key_pool.shape, BF16),
                 pltpu.VMEM(value_pool.shape, BF16),
-                pltpu.VMEM((planes + 1, micros * heads, LANES), F32),
-                pltpu.VMEM((planes + 1, micros * heads, LANES), F32),
-                pltpu.VMEM((planes + 1, 8, LANES), F32),
+                *[pltpu.VMEM((planes + 1, micros, heads, LANES), F32)] * 4,
+                pltpu.VMEM((planes + 1, micros, 8, LANES), F32),
                 pltpu.VMEM((planes, 2, LANES), F32),
                 pltpu.SMEM((8, LANES), jnp.int32),
                 pltpu.SemaphoreType.DMA((2,)),

time: 78.9 us -> 78.1 us (0.990)
  no operation moved by 1% of the time
where the time goes in v6:
time: 78.1 us; the launch traced here: 77.7 us
  blocking collectives  33.1 us (42%)
  starting transfers between devices  20.9 us (27%)
  waiting for transfers between devices  14.3 us (18%)
  Pallas kernels  9.28 us (12%)
    all_to_all x2, blocking collectives, exchange(): return lax.all_to_all(x, axis, 0, 0)  33.1 us
    all_to_all x1, starting transfers between devices, exchange(): return lax.all_to_all(x, axis, 0, 0)  16.6 us
    all_to_all x1, waiting for transfers between devices, exchange(): return lax.all_to_all(x, axis, 0, 0)  14.3 us
    pallas_call x1, Pallas kernels, per_device(): pl.pallas_call(functools.partial(holder_kernel, heads, scale), out_shape=...  5.56 us
    ppermute x1, starting transfers between devices, per_device(): sib_value = lax.ppermute(value_pool, 'c', swap)  2.41 us
    ppermute x1, starting transfers between devices, per_device(): sib_key = lax.ppermute(key_pool, 'c', swap)  1.92 us
  transfers between devices with their start and end apart: 3, of which 1 were waited for; matrix products, arithmetic and copies ran while one was open for 0% of the time, Pallas kernels for 0%

profile of v6, /device:TPU:8, one launch (start us, length us, event | category | flops | bytes accessed | tf_op | source)
XLA Modules:
  0.0 77.7 jit_solution(825008904752903585)
XLA Ops:
  0.0 0.8 queries_to_holders.2
  0.8 9.4 %all_to_all.15.list_ref = s32[4,2,2,8]{3,2,1,0:T(2,128)S(1)} all-to-all(s32[4,2,2,8]{3,2,1,0:T(2,128)S(1)} %get-tuple-element.9), channel_id=1, replica_groups=mesh['zy'=64,'c'=2,'tp'=4] {'tp'}, dimensions={0} | all-to-all | bytes 1024 | tf_op jit(solution)/shard_map/queries_to_holders/all_to_all | solution.py:287
  10.2 1.1 %queries_to_holders.3 = bf16[64,17,2,128]{3,2,1,0:T(2,128)(2,1)} custom-call(bf16[16,2,128]{2,1,0:T(2,128)(2,1)S(1)} %get-tuple-element.8.query_ref, s32[4,2,2,8]{3,2,1,0:T(2,128)S(1)} %all_to_all.15.list_ref, f32[8,128]{1,0:T(8,128)S(1)} %get-tuple-element.10.tail_ref), custom_call_target="tpu_custom_call" | custom-call | tf_op jit(solution)/shard_map/queries_to_holders/pallas_call | solution.py:327
  11.3 16.6 %all-to-all-start.1 = ((bf16[64,17,2,128]{3,2,1,0:T(2,128)(2,1)}), bf16[64,17,2,128]{3,2,1,0:T(2,128)(2,1)S(1)}, u32[]{:S(2)}, u32[]{:S(2)}) async-start(bf16[64,17,2,128]{3,2,1,0:T(2,128)(2,1)} %queries_to_holders.3), calls=%async_computation.1 | async-start | bytes 1114112 | tf_op jit(solution)/shard_map/queries_to_holders/all_to_all | solution.py:287
  27.9 1.9 %collective-permute-start = (bf16[64,128,128]{2,1,0:T(8,128)(2,1)}, bf16[64,128,128]{2,1,0:T(8,128)(2,1)S(1)}, u32[]{:S(2)}, u32[]{:S(2)}) collective-permute-start(bf16[64,128,128]{2,1,0:T(8,128)(2,1)} %key_ref.1), channel_id=1, source_target_pairs={{0,4},{4,0},{1,5},{5,1},{2,6},{6,2},{3,7},{7,3},{8,12},{12,8},{9,1... | collective-permute-start | bytes 6291464 | tf_op jit(solution)/shard_map/pools_of_both_cores/ppermute | solution.py:337
  29.8 2.4 %collective-permute-start.1 = (bf16[64,128,128]{2,1,0:T(8,128)(2,1)}, bf16[64,128,128]{2,1,0:T(8,128)(2,1)}, u32[]{:S(2)}, u32[]{:S(2)}) collective-permute-start(bf16[64,128,128]{2,1,0:T(8,128)(2,1)} %value_ref.1), channel_id=1, source_target_pairs={{0,4},{4,0},{1,5},{5,1},{2,6},{6,2},{3,7},{7,3},{8,12},{12,8},{9,1... | collective-permute-start | bytes 6291464 | tf_op jit(solution)/shard_map/pools_of_both_cores/ppermute | solution.py:338
  32.3 14.3 %all-to-all-done.1.own_ref = bf16[64,17,2,128]{3,2,1,0:T(2,128)(2,1)S(1)} async-done(((bf16[64,17,2,128]{3,2,1,0:T(2,128)(2,1)}), bf16[64,17,2,128]{3,2,1,0:T(2,128)(2,1)S(1)}, u32[]{:S(2)}, u32[]{:S(2)}) %all-to-all-start.1) | async-done | bytes 557088 | tf_op jit(solution)/shard_map/queries_to_holders/all_to_all | solution.py:287
  46.6 0.4 block_attention.2.found_ref
  46.9 0.0 copy-start
  47.0 0.0 copy-start.1
  47.0 0.0 copy-start.2
  47.0 0.0 collective-permute-done.sib_key_ref
  47.0 0.0 collective-permute-done.1.sib_value_ref
  47.0 5.6 %block_attention.3 = bf16[64,17,2,128]{3,2,1,0:T(2,128)(2,1)S(1)} custom-call(bf16[64,17,2,128]{3,2,1,0:T(2,128)(2,1)S(1)} %all-to-all-done.1.own_ref, s32[8,128]{1,0:T(8,128)S(1)} %block_attention.2.found_ref, bf16[64,128,128]{2,1,0:T(8,128)(2,1)} %key_ref.1, bf16[64,128,128]{2,1,0:T(8,128)(2,1)} %value_ref.1, ...), custom_call_target="tpu_custom_call" | custom-call | tf_op jit(solution)/shard_map/block_attention/pallas_call | solution.py:352
  52.6 23.7 %all_to_all.16.part_ref = bf16[64,17,2,128]{3,2,1,0:T(2,128)(2,1)S(1)} all-to-all(bf16[64,17,2,128]{3,2,1,0:T(2,128)(2,1)S(1)} %block_attention.3), channel_id=1, replica_groups=mesh['zy'=64,'c'=2,'tp'=4] {'zy'}, dimensions={0} | all-to-all | bytes 1114112 | tf_op jit(solution)/shard_map/parts_to_owners/all_to_all | solution.py:287
  76.3 0.0 copy-done
  76.3 0.0 copy-done.1
  76.3 0.0 copy-done.2
  76.3 1.5 %owner_sum.1 = bf16[16,2,128]{2,1,0:T(2,128)(2,1)} custom-call(bf16[64,17,2,128]{3,2,1,0:T(2,128)(2,1)S(1)} %all_to_all.16.part_ref, bf16[16,2,128]{2,1,0:T(2,128)(2,1)S(1)} %bitcast.12, bf16[2,128]{1,0:T(2,128)(2,1)S(1)} %bitcast.13, bf16[2,128]{1,0:T(2,128)(2,1)S(1)} %bitcast.14), custom_call_target="tpu_custom_call" | custom-call | tf_op jit(solution)/shard_map/owner_sum/pallas_call | solution.py:372
Async XLA Ops:
  11.3 35.3 %all-to-all-start.1 = ((bf16[64,17,2,128]{3,2,1,0:T(2,128)(2,1)}), bf16[64,17,2,128]{3,2,1,0:T(2,128)(2,1)S(1)}, u32[]{:S(2)}, u32[]{:S(2)}) async-start(bf16[64,17,2,128]{3,2,1,0:T(2,128)(2,1)} %queries_to_holders.3), calls=%async_computation.1 | async-start | bytes 1114112 | tf_op jit(solution)/shard_map/queries_to_holders/all_to_all | solution.py:287
  27.9 19.1 %collective-permute-start = (bf16[64,128,128]{2,1,0:T(8,128)(2,1)}, bf16[64,128,128]{2,1,0:T(8,128)(2,1)S(1)}, u32[]{:S(2)}, u32[]{:S(2)}) collective-permute-start(bf16[64,128,128]{2,1,0:T(8,128)(2,1)} %key_ref.1), channel_id=1, source_target_pairs={{0,4},{4,0},{1,5},{5,1},{2,6},{6,2},{3,7},{7,3},{8,12},{12,8},{9,1... | collective-permute-start | bytes 6291464 | tf_op jit(solution)/shard_map/pools_of_both_cores/ppermute | solution.py:337
  29.8 17.2 %collective-permute-start.1 = (bf16[64,128,128]{2,1,0:T(8,128)(2,1)}, bf16[64,128,128]{2,1,0:T(8,128)(2,1)}, u32[]{:S(2)}, u32[]{:S(2)}) collective-permute-start(bf16[64,128,128]{2,1,0:T(8,128)(2,1)} %value_ref.1), channel_id=1, source_target_pairs={{0,4},{4,0},{1,5},{5,1},{2,6},{6,2},{3,7},{7,3},{8,12},{12,8},{9,1... | collective-permute-start | bytes 6291464 | tf_op jit(solution)/shard_map/pools_of_both_cores/ppermute | solution.py:338
  46.9 29.3 %copy-start = (bf16[2,1,2048]{2,0,1:T(2,128)(2,1)S(1)}, bf16[2,1,2048]{2,0,1:T(2,128)(2,1)}, u32[]{:S(2)}) copy-start(bf16[2,1,2048]{2,0,1:T(2,128)(2,1)} %param.7) | copy-start | bytes 24580
  47.0 29.3 %copy-start.1 = (bf16[2,1,128]{2,0,1:T(2,128)(2,1)S(1)}, bf16[2,1,128]{2,0,1:T(2,128)(2,1)}, u32[]{:S(2)}) copy-start(bf16[2,1,128]{2,0,1:T(2,128)(2,1)} %param.8) | copy-start | bytes 1540
  47.0 29.3 %copy-start.2 = (bf16[2,1,128]{2,0,1:T(2,128)(2,1)S(1)}, bf16[2,1,128]{2,0,1:T(2,128)(2,1)}, u32[]{:S(2)}) copy-start(bf16[2,1,128]{2,0,1:T(2,128)(2,1)} %param.9) | copy-start | bytes 1540

commit v7 on v6

--- a/solution.py
+++ b/solution.py
@@ -154,7 +154,7 @@
     tops[...] = jnp.full(tops.shape, EMPTY, F32)
     sums[...] = jnp.zeros(sums.shape, F32)
     mixed[...] = jnp.zeros(mixed.shape, F32)
-    parts[...] = jnp.zeros(parts.shape, F32)
+    parts[...] = jnp.zeros(parts.shape, BF16)
     pad[...] = jnp.zeros(pad.shape, F32)
     lane8 = lane_ids((8, LANES))
     sublane = lax.broadcasted_iota(jnp.int32, (8, LANES), 0)
@@ -236,7 +236,8 @@
                 tops[where, micro] = top
                 sums[where, micro] = new_sum
                 mixed[where, micro] = new_mixed
-                parts[where, micro] = part
+                inner = pl.ds(micro * (heads // 2), heads // 2)
+                parts[where, inner] = part.astype(BF16).reshape(heads // 2, 2, LANES)
                 tiles[where, micro] = tile
         return carry
 
@@ -250,7 +251,7 @@
 
     pad[:, 0, :] = jnp.sum(tiles[:ranks, 0] + tiles[:ranks, 1], axis=1)
     out_ref[:, heads] = pad[...].astype(BF16)
-    out_ref[:, :heads] = parts[:ranks].astype(BF16).reshape(ranks, heads, 2, LANES)
+    out_ref[:, :heads] = parts[:ranks]
 
 
 def owner_kernel(heads, scale, part_ref, query_ref, key_ref, value_ref, out_ref, wide):
@@ -357,7 +358,8 @@
             scratch_shapes=[
                 pltpu.VMEM(key_pool.shape, BF16),
                 pltpu.VMEM(value_pool.shape, BF16),
-                *[pltpu.VMEM((planes + 1, micros, heads, LANES), F32)] * 4,
+                *[pltpu.VMEM((planes + 1, micros, heads, LANES), F32)] * 3,
+                pltpu.VMEM((planes + 1, heads, micros, LANES), BF16),
                 pltpu.VMEM((planes + 1, micros, 8, LANES), F32),
                 pltpu.VMEM((planes, 2, LANES), F32),
                 pltpu.SMEM((8, LANES), jnp.int32),

time: 78.1 us -> 77.8 us (level)
  no operation moved by 1% of the time
where the time goes in v7:
time: 77.8 us; the launch traced here: 77.5 us
  blocking collectives  33.1 us (43%)
  starting transfers between devices  20.9 us (27%)
  waiting for transfers between devices  14.3 us (18%)
  Pallas kernels  9 us (12%)
    all_to_all x2, blocking collectives, exchange(): return lax.all_to_all(x, axis, 0, 0)  33.1 us
    all_to_all x1, starting transfers between devices, exchange(): return lax.all_to_all(x, axis, 0, 0)  16.6 us
    all_to_all x1, waiting for transfers between devices, exchange(): return lax.all_to_all(x, axis, 0, 0)  14.3 us
    pallas_call x1, Pallas kernels, per_device(): pl.pallas_call(functools.partial(holder_kernel, heads, scale), out_shape=...  5.29 us
    ppermute x1, starting transfers between devices, per_device(): sib_value = lax.ppermute(value_pool, 'c', swap)  2.41 us
    ppermute x1, starting transfers between devices, per_device(): sib_key = lax.ppermute(key_pool, 'c', swap)  1.92 us
  transfers between devices with their start and end apart: 3, of which 1 were waited for; matrix products, arithmetic and copies ran while one was open for 0% of the time, Pallas kernels for 0%

profile of v7, /device:TPU:8, one launch (start us, length us, event | category | flops | bytes accessed | tf_op | source)
XLA Modules:
  0.0 77.5 jit_solution(4983049725313748094)
XLA Ops:
  0.0 0.8 %queries_to_holders.2 = (s32[4,2,2,8]{3,2,1,0:T(2,128)S(1)}, bf16[16,2,128]{2,1,0:T(2,128)(2,1)S(1)}, f32[8,128]{1,0:T(8,128)S(1)}) custom-call(bf16[16,2,128]{2,1,0:T(2,128)(2,1)} %bitcast.11, s32[2,2,8]{2,1,0:T(2,128)} %bitcast.15, s32[1,2]{1,0:T(1,128)} %bitcast.16), custom_call_target="tpu_custom_call" | custom-call | tf_op jit(solution)/shard_map/queries_to_holders/pallas_call | solution.py:309
  0.8 9.4 %all_to_all.15.list_ref = s32[4,2,2,8]{3,2,1,0:T(2,128)S(1)} all-to-all(s32[4,2,2,8]{3,2,1,0:T(2,128)S(1)} %get-tuple-element.9), channel_id=1, replica_groups=mesh['zy'=64,'c'=2,'tp'=4] {'tp'}, dimensions={0} | all-to-all | bytes 1024 | tf_op jit(solution)/shard_map/queries_to_holders/all_to_all | solution.py:288
  10.2 1.1 %queries_to_holders.3 = bf16[64,17,2,128]{3,2,1,0:T(2,128)(2,1)} custom-call(bf16[16,2,128]{2,1,0:T(2,128)(2,1)S(1)} %get-tuple-element.8.query_ref, s32[4,2,2,8]{3,2,1,0:T(2,128)S(1)} %all_to_all.15.list_ref, f32[8,128]{1,0:T(8,128)S(1)} %get-tuple-element.10.tail_ref), custom_call_target="tpu_custom_call" | custom-call | tf_op jit(solution)/shard_map/queries_to_holders/pallas_call | solution.py:328
  11.3 16.6 %all-to-all-start.1 = ((bf16[64,17,2,128]{3,2,1,0:T(2,128)(2,1)}), bf16[64,17,2,128]{3,2,1,0:T(2,128)(2,1)S(1)}, u32[]{:S(2)}, u32[]{:S(2)}) async-start(bf16[64,17,2,128]{3,2,1,0:T(2,128)(2,1)} %queries_to_holders.3), calls=%async_computation.1 | async-start | bytes 1114112 | tf_op jit(solution)/shard_map/queries_to_holders/all_to_all | solution.py:288
  27.9 1.9 %collective-permute-start = (bf16[64,128,128]{2,1,0:T(8,128)(2,1)}, bf16[64,128,128]{2,1,0:T(8,128)(2,1)S(1)}, u32[]{:S(2)}, u32[]{:S(2)}) collective-permute-start(bf16[64,128,128]{2,1,0:T(8,128)(2,1)} %key_ref.1), channel_id=1, source_target_pairs={{0,4},{4,0},{1,5},{5,1},{2,6},{6,2},{3,7},{7,3},{8,12},{12,8},{9,1... | collective-permute-start | bytes 6291464 | tf_op jit(solution)/shard_map/pools_of_both_cores/ppermute | solution.py:338
  29.8 2.4 %collective-permute-start.1 = (bf16[64,128,128]{2,1,0:T(8,128)(2,1)}, bf16[64,128,128]{2,1,0:T(8,128)(2,1)}, u32[]{:S(2)}, u32[]{:S(2)}) collective-permute-start(bf16[64,128,128]{2,1,0:T(8,128)(2,1)} %value_ref.1), channel_id=1, source_target_pairs={{0,4},{4,0},{1,5},{5,1},{2,6},{6,2},{3,7},{7,3},{8,12},{12,8},{9,1... | collective-permute-start | bytes 6291464 | tf_op jit(solution)/shard_map/pools_of_both_cores/ppermute | solution.py:339
  32.3 14.3 %all-to-all-done.1.own_ref = bf16[64,17,2,128]{3,2,1,0:T(2,128)(2,1)S(1)} async-done(((bf16[64,17,2,128]{3,2,1,0:T(2,128)(2,1)}), bf16[64,17,2,128]{3,2,1,0:T(2,128)(2,1)S(1)}, u32[]{:S(2)}, u32[]{:S(2)}) %all-to-all-start.1) | async-done | bytes 557088 | tf_op jit(solution)/shard_map/queries_to_holders/all_to_all | solution.py:288
  46.6 0.4 block_attention.2.found_ref
  46.9 0.0 copy-start
  47.0 0.0 copy-start.1
  47.0 0.0 copy-start.2
  47.0 0.0 collective-permute-done.sib_key_ref
  47.0 0.0 collective-permute-done.1.sib_value_ref
  47.0 5.3 %block_attention.3 = bf16[64,17,2,128]{3,2,1,0:T(2,128)(2,1)S(1)} custom-call(bf16[64,17,2,128]{3,2,1,0:T(2,128)(2,1)S(1)} %all-to-all-done.1.own_ref, s32[8,128]{1,0:T(8,128)S(1)} %block_attention.2.found_ref, bf16[64,128,128]{2,1,0:T(8,128)(2,1)} %key_ref.1, bf16[64,128,128]{2,1,0:T(8,128)(2,1)} %value_ref.1, ...), custom_call_target="tpu_custom_call" | custom-call | tf_op jit(solution)/shard_map/block_attention/pallas_call | solution.py:353
  52.3 23.7 %all_to_all.16.part_ref = bf16[64,17,2,128]{3,2,1,0:T(2,128)(2,1)S(1)} all-to-all(bf16[64,17,2,128]{3,2,1,0:T(2,128)(2,1)S(1)} %block_attention.3), channel_id=1, replica_groups=mesh['zy'=64,'c'=2,'tp'=4] {'zy'}, dimensions={0} | all-to-all | bytes 1114112 | tf_op jit(solution)/shard_map/parts_to_owners/all_to_all | solution.py:288
  76.0 0.0 copy-done
  76.0 0.0 copy-done.1
  76.0 0.0 copy-done.2
  76.0 1.5 %owner_sum.1 = bf16[16,2,128]{2,1,0:T(2,128)(2,1)} custom-call(bf16[64,17,2,128]{3,2,1,0:T(2,128)(2,1)S(1)} %all_to_all.16.part_ref, bf16[16,2,128]{2,1,0:T(2,128)(2,1)S(1)} %bitcast.12, bf16[2,128]{1,0:T(2,128)(2,1)S(1)} %bitcast.13, bf16[2,128]{1,0:T(2,128)(2,1)S(1)} %bitcast.14), custom_call_target="tpu_custom_call" | custom-call | tf_op jit(solution)/shard_map/owner_sum/pallas_call | solution.py:374
Async XLA Ops:
  11.3 35.3 %all-to-all-start.1 = ((bf16[64,17,2,128]{3,2,1,0:T(2,128)(2,1)}), bf16[64,17,2,128]{3,2,1,0:T(2,128)(2,1)S(1)}, u32[]{:S(2)}, u32[]{:S(2)}) async-start(bf16[64,17,2,128]{3,2,1,0:T(2,128)(2,1)} %queries_to_holders.3), calls=%async_computation.1 | async-start | bytes 1114112 | tf_op jit(solution)/shard_map/queries_to_holders/all_to_all | solution.py:288
  27.9 19.1 %collective-permute-start = (bf16[64,128,128]{2,1,0:T(8,128)(2,1)}, bf16[64,128,128]{2,1,0:T(8,128)(2,1)S(1)}, u32[]{:S(2)}, u32[]{:S(2)}) collective-permute-start(bf16[64,128,128]{2,1,0:T(8,128)(2,1)} %key_ref.1), channel_id=1, source_target_pairs={{0,4},{4,0},{1,5},{5,1},{2,6},{6,2},{3,7},{7,3},{8,12},{12,8},{9,1... | collective-permute-start | bytes 6291464 | tf_op jit(solution)/shard_map/pools_of_both_cores/ppermute | solution.py:338
  29.8 17.2 %collective-permute-start.1 = (bf16[64,128,128]{2,1,0:T(8,128)(2,1)}, bf16[64,128,128]{2,1,0:T(8,128)(2,1)}, u32[]{:S(2)}, u32[]{:S(2)}) collective-permute-start(bf16[64,128,128]{2,1,0:T(8,128)(2,1)} %value_ref.1), channel_id=1, source_target_pairs={{0,4},{4,0},{1,5},{5,1},{2,6},{6,2},{3,7},{7,3},{8,12},{12,8},{9,1... | collective-permute-start | bytes 6291464 | tf_op jit(solution)/shard_map/pools_of_both_cores/ppermute | solution.py:339
  46.9 29.1 %copy-start = (bf16[2,1,2048]{2,0,1:T(2,128)(2,1)S(1)}, bf16[2,1,2048]{2,0,1:T(2,128)(2,1)}, u32[]{:S(2)}) copy-start(bf16[2,1,2048]{2,0,1:T(2,128)(2,1)} %param.7) | copy-start | bytes 24580
  47.0 29.0 %copy-start.1 = (bf16[2,1,128]{2,0,1:T(2,128)(2,1)S(1)}, bf16[2,1,128]{2,0,1:T(2,128)(2,1)}, u32[]{:S(2)}) copy-start(bf16[2,1,128]{2,0,1:T(2,128)(2,1)} %param.8) | copy-start | bytes 1540
  47.0 29.0 %copy-start.2 = (bf16[2,1,128]{2,0,1:T(2,128)(2,1)S(1)}, bf16[2,1,128]{2,0,1:T(2,128)(2,1)}, u32[]{:S(2)}) copy-start(bf16[2,1,128]{2,0,1:T(2,128)(2,1)} %param.9) | copy-start | bytes 1540
